TPU v7x, 32 devices: a whole 2x2x4 slice. The times are simulated.
32 devices in a mesh: dp: 8 (over z, y), mp: 4 (over x, core).
Axes of the slice: x: 2, y: 2, z: 4, core: 2. Of those that a mesh axis runs over, the one named last changes fastest.
Arguments:
- latents: bfloat16 [16, 1024, 768], P('dp', 'mp'), may hold values from -6 to 6
- conditions: bfloat16 [16, 768], P('dp'), may hold values from -6 to 6
- cotangent: bfloat16 [16, 1024, 768], P('dp', 'mp'), may hold values from -6 to 6
- counts: int32 [8], P('dp'), may hold values from 1 to 2, as said below
- w_mod: float32 [768, 4608], P('dp'), may hold values from -0.21875 to 0.21875
- mom_mod: float32 [768, 4608], P('dp'), may hold values from -32 to 32
- conv_attn: float32 [9, 768], replicated, may hold values from -2 to 2
- mom_conv_attn: float32 [9, 768], replicated, may hold values from -24 to 24
- w_qkv: float32 [3, 768, 768], P(None, None, 'mp'), may hold values from -0.21875 to 0.21875
- mom_qkv: float32 [3, 768, 768], P(None, None, 'mp'), may hold values from -12 to 12
- err_qkv: float32 [8, 3, 768, 768], P('dp', None, None, 'mp'), may hold values from -32 to 32
- start_qkv: float32 [3, 768, 8], P(None, 'mp'), may hold values from -6 to 6
- w_out: float32 [768, 768], P('mp'), may hold values from -1.75 to 1.75
- mom_out: float32 [768, 768], P('mp'), may hold values from -4 to 4
- err_out: float32 [8, 768, 768], P('dp', 'mp'), may hold values from -12 to 12
- start_out: float32 [768, 8], replicated, may hold values from -6 to 6
- w_fc1: float32 [768, 3072], P(None, 'mp'), may hold values from -0.21875 to 0.21875
- mom_fc1: float32 [768, 3072], P(None, 'mp'), may hold values from -16 to 16
- err_fc1: float32 [8, 768, 3072], P('dp', None, 'mp'), may hold values from -48 to 48
- start_fc1: float32 [3072, 8], P('mp'), may hold values from -6 to 6
- conv_ffn: float32 [9, 3072], P(None, 'mp'), may hold values from -2 to 2
- mom_conv_ffn: float32 [9, 3072], P(None, 'mp'), may hold values from -16 to 16
- w_fc2: float32 [3072, 768], P('mp'), may hold values from -0.109375 to 0.109375
- mom_fc2: float32 [3072, 768], P('mp'), may hold values from -28 to 28
- err_fc2: float32 [8, 3072, 768], P('dp', 'mp'), may hold values from -80 to 80
- start_fc2: float32 [768, 8], replicated, may hold values from -6 to 6
Outputs:
- latents_out: bfloat16 [16, 1024, 768], P('dp', 'mp')
- latents_grad: bfloat16 [16, 1024, 768], P('dp', 'mp')
- w_mod_new: float32 [768, 4608], P('dp')
- mom_mod_new: float32 [768, 4608], P('dp')
- conv_attn_new: float32 [9, 768], replicated
- mom_conv_attn_new: float32 [9, 768], replicated
- w_qkv_new: float32 [3, 768, 768], P(None, None, 'mp')
- mom_qkv_new: float32 [3, 768, 768], P(None, None, 'mp')
- err_qkv_new: float32 [8, 3, 768, 768], P('dp', None, None, 'mp')
- w_out_new: float32 [768, 768], P('mp')
- mom_out_new: float32 [768, 768], P('mp')
- err_out_new: float32 [8, 768, 768], P('dp', 'mp')
- w_fc1_new: float32 [768, 3072], P(None, 'mp')
- mom_fc1_new: float32 [768, 3072], P(None, 'mp')
- err_fc1_new: float32 [8, 768, 3072], P('dp', None, 'mp')
- conv_ffn_new: float32 [9, 3072], P(None, 'mp')
- mom_conv_ffn_new: float32 [9, 3072], P(None, 'mp')
- w_fc2_new: float32 [3072, 768], P('mp')
- mom_fc2_new: float32 [3072, 768], P('mp')
- err_fc2_new: float32 [8, 3072, 768], P('dp', 'mp')
Inputs may be any that keep to these rules, and one draw needn't show every extreme that they name: Index d of dp holds live latents in its first counts[d] slots; the others are padding. Some index holds 2 and some holds 1.
All inputs are finite; a program needn't handle non-finite values.
Results may differ from a plain program's by a relative error of at most 0.023.
Values may be sent and summed in bfloat16 or wider, within the bound.
No kernel may reach another device: no remote copies, remote signals or barrier semaphores. Data moves between devices by JAX's collectives and lax.ppermute only.
A program may use at most 320 MiB of HBM per device.

v0:
```python
import jax
import jax.numpy as jnp
from jax import lax
from jax.sharding import PartitionSpec as P

HEAD_DIM = 64
SIDE = 32


NORM_EPS = 1e-06
ORTHO_EPS = 1e-06
LEARN_RATE = 0.005
FAST_RATE = 0.025
MOMENTUM = 0.9
HIGHEST = lax.Precision.HIGHEST


def layer_norm(values):
    centred = values - jnp.mean(values, -1, keepdims=True)
    variance = jnp.mean(centred * centred, -1, keepdims=True)
    return centred * lax.rsqrt(variance + NORM_EPS)


def conv_grid(values, kernel):
    channels = values.shape[-1]
    padded = jnp.pad(values.reshape(SIDE, SIDE, channels), ((1, 1), (1, 1), (0, 0)))
    summed = jnp.zeros((SIDE, SIDE, channels), jnp.float32)
    for vertical in range(3):
        for lateral in range(3):
            summed = (
                summed
                + kernel[3 * vertical + lateral]
                * padded[vertical : vertical + SIDE, lateral : lateral + SIDE]
            )
    return summed.reshape(SIDE * SIDE, channels)


def conv_back_rows(grad_ext, shifted_ext, kernel, grid_rows):
    channels = grad_ext.shape[-1]
    grad_grid = grad_ext.reshape(grid_rows + 2, SIDE, channels)
    grad_pad = jnp.pad(grad_grid, ((0, 0), (1, 1), (0, 0)))
    shift_pad = jnp.pad(
        shifted_ext.reshape(grid_rows + 2, SIDE, channels), ((0, 0), (1, 1), (0, 0))
    )
    grad_mid = grad_grid[1 : grid_rows + 1]
    summed = jnp.zeros((grid_rows, SIDE, channels), jnp.float32)
    kernel_terms = []
    for vertical in range(3):
        for lateral in range(3):
            summed = (
                summed
                + kernel[3 * vertical + lateral]
                * grad_pad[
                    2 - vertical : 2 - vertical + grid_rows, 2 - lateral : 2 - lateral + SIDE
                ]
            )
            kernel_terms.append(
                jnp.sum(
                    shift_pad[vertical : vertical + grid_rows, lateral : lateral + SIDE] * grad_mid,
                    (0, 1),
                )
            )
    return (summed.reshape(grid_rows * SIDE, channels), jnp.stack(kernel_terms))


def gelu_tanh(values):
    return jax.nn.gelu(values, approximate=True)


def to_groups(values):
    channels = values.shape[-1]
    shaped = values.reshape(SIDE // 2, 2, SIDE // 2, 2, channels).transpose(1, 3, 0, 2, 4)
    return shaped.reshape(4, (SIDE // 2) ** 2, channels)


def from_groups(values):
    channels = values.shape[-1]
    shaped = values.reshape(2, 2, SIDE // 2, SIDE // 2, channels).transpose(2, 0, 3, 1, 4)
    return shaped.reshape(SIDE * SIDE, channels)


def split_heads(values, head_count):
    return to_groups(values).reshape(4, -1, head_count, HEAD_DIM)


def join_heads(values):
    return from_groups(values.reshape(values.shape[0], values.shape[1], -1))


def orthonormal(factor):
    columns = []
    for column in range(factor.shape[-1]):
        current = factor[..., column]
        for earlier in columns:
            current = current - jnp.sum(earlier * current, -1, keepdims=True) * earlier
        current = current * lax.rsqrt(jnp.sum(current * current, -1, keepdims=True) + ORTHO_EPS)
        columns.append(current)
    return jnp.stack(columns, -1)


def momentum_update(weight, moment, gradient, rate):
    new_moment = MOMENTUM * moment + gradient
    return (weight - rate * new_moment, new_moment)


def share_of(values, begin, share):
    return lax.dynamic_slice_in_dim(values, begin, share, 0)


def per_device(
    latents,
    conditions,
    cotangent,
    counts,
    w_mod,
    mom_mod,
    conv_attn,
    mom_conv_attn,
    w_qkv,
    mom_qkv,
    err_qkv,
    start_qkv,
    w_out,
    mom_out,
    err_out,
    start_out,
    w_fc1,
    mom_fc1,
    err_fc1,
    start_fc1,
    conv_ffn,
    mom_conv_ffn,
    w_fc2,
    mom_fc2,
    err_fc2,
    start_fc2,
):
    slots = latents.shape[0]
    share = latents.shape[1]
    model_width = latents.shape[2]
    grid_rows = share // SIDE
    heads_local = w_qkv.shape[2] // HEAD_DIM
    score_scale = HEAD_DIM ** (-0.5)
    begin = lax.axis_index("mp") * share
    begin_row = lax.axis_index("mp") * grid_rows
    dp_count = lax.axis_size("dp")
    mod_weight = lax.all_gather(w_mod.astype(jnp.bfloat16), "dp", axis=0, tiled=True)
    silu_cond = jax.nn.silu(conditions.astype(jnp.float32)).astype(jnp.bfloat16)
    modulation = jnp.dot(silu_cond, mod_weight, preferred_element_type=jnp.float32).reshape(
        slots, 6, model_width
    )
    full_latents, full_cotangent = (
        lax.all_gather(latents, "mp", axis=1, tiled=True),
        lax.all_gather(cotangent, "mp", axis=1, tiled=True),
    )
    qkv_low = w_qkv.astype(jnp.bfloat16)
    out_low = w_out.astype(jnp.bfloat16)
    fc1_low = w_fc1.astype(jnp.bfloat16)
    fc2_low = w_fc2.astype(jnp.bfloat16)
    grad_qkv = jnp.zeros(w_qkv.shape, jnp.float32)
    grad_out = jnp.zeros(w_out.shape, jnp.float32)
    grad_fc1 = jnp.zeros(w_fc1.shape, jnp.float32)
    grad_fc2 = jnp.zeros(w_fc2.shape, jnp.float32)
    grad_conv_attn = jnp.zeros(conv_attn.shape, jnp.float32)
    grad_conv_ffn = jnp.zeros(conv_ffn.shape, jnp.float32)
    mod_parts = []
    outputs = []
    input_grads = []
    for slot in range(slots):
        live_mask = (counts[0] > slot).astype(jnp.float32)
        shift_one = modulation[slot, 0]
        scale_one = modulation[slot, 1]
        gate_one = modulation[slot, 2]
        shift_two = modulation[slot, 3]
        scale_two = modulation[slot, 4]
        gate_two = modulation[slot, 5]
        inputs_full = full_latents[slot].astype(jnp.float32)
        inputs_share = latents[slot].astype(jnp.float32)
        normed_one = layer_norm(inputs_full)
        shifted = normed_one * (1.0 + scale_one) + shift_one
        conv_low = conv_grid(shifted, conv_attn).astype(jnp.bfloat16)
        projected = jnp.einsum(
            "ld,tde->tle", conv_low, qkv_low, preferred_element_type=jnp.float32
        ).astype(jnp.bfloat16)
        query = split_heads(projected[0], heads_local)
        keyed = split_heads(projected[1], heads_local)
        valued = split_heads(projected[2], heads_local)
        scores = (
            jnp.einsum("aqhe,akhe->ahqk", query, keyed, preferred_element_type=jnp.float32)
            * score_scale
        )
        log_total = jax.nn.logsumexp(scores, -1, keepdims=True)
        probs = jnp.exp(scores - log_total)
        attended_g = jnp.einsum(
            "ahqk,akhe->aqhe",
            probs.astype(jnp.bfloat16),
            valued,
            preferred_element_type=jnp.float32,
        )
        attended = join_heads(attended_g.astype(jnp.bfloat16))
        attn_part = jnp.dot(attended, out_low, preferred_element_type=jnp.float32)
        attn_full = lax.psum(attn_part.astype(jnp.bfloat16), "mp").astype(jnp.float32)
        resid_full = inputs_full + gate_one * attn_full
        normed_full = layer_norm(resid_full)
        mixed_low = (normed_full * (1.0 + scale_two) + shift_two).astype(jnp.bfloat16)
        attn_share = share_of(attn_full, begin, share)
        resid_share = share_of(resid_full, begin, share)
        normed_two = share_of(normed_full, begin, share)
        hidden = jnp.dot(mixed_low, fc1_low, preferred_element_type=jnp.float32)
        pre_act = conv_grid(hidden, conv_ffn)
        activated, gelu_back = jax.vjp(gelu_tanh, pre_act)
        act_low = activated.astype(jnp.bfloat16)
        ffn_part = jnp.dot(act_low, fc2_low, preferred_element_type=jnp.float32)
        ffn_share = lax.psum_scatter(
            ffn_part.astype(jnp.bfloat16), "mp", scatter_dimension=0, tiled=True
        ).astype(jnp.float32)
        outputs.append((live_mask * (resid_share + gate_two * ffn_share)).astype(jnp.bfloat16))
        grad_full = live_mask * full_cotangent[slot].astype(jnp.float32)
        grad_share = share_of(grad_full, begin, share)
        ffn_grad_low = (gate_two * grad_full).astype(jnp.bfloat16)
        grad_fc2 = grad_fc2 + jnp.einsum(
            "lf,ld->fd", act_low, ffn_grad_low, preferred_element_type=jnp.float32
        )
        act_grad = jnp.einsum(
            "ld,fd->lf", ffn_grad_low, fc2_low, preferred_element_type=jnp.float32
        )
        (pre_grad,) = gelu_back(act_grad)
        conv_out_ffn, ffn_conv_back = jax.vjp(conv_grid, hidden, conv_ffn)
        hidden_grad, kernel_ffn_grad = ffn_conv_back(pre_grad)
        grad_conv_ffn = grad_conv_ffn + kernel_ffn_grad
        hidden_grad_low = hidden_grad.astype(jnp.bfloat16)
        grad_fc1 = grad_fc1 + jnp.einsum(
            "ld,lf->df", mixed_low, hidden_grad_low, preferred_element_type=jnp.float32
        )
        mixed_part = jnp.einsum(
            "lf,df->ld", hidden_grad_low, fc1_low, preferred_element_type=jnp.float32
        )
        mixed_full = lax.psum(mixed_part.astype(jnp.bfloat16), "mp").astype(jnp.float32)
        normed_again, second_back = jax.vjp(layer_norm, resid_full)
        (resid_norm_grad,) = second_back(mixed_full * (1.0 + scale_two))
        resid_grad_full = grad_full + resid_norm_grad
        attn_grad_low = (gate_one * resid_grad_full).astype(jnp.bfloat16)
        mixed_grad = share_of(mixed_full, begin, share)
        resid_grad = share_of(resid_grad_full, begin, share)
        grad_out = grad_out + jnp.einsum(
            "lc,ld->cd", attended, attn_grad_low, preferred_element_type=jnp.float32
        )
        attended_grad = jnp.einsum(
            "ld,cd->lc", attn_grad_low, out_low, preferred_element_type=jnp.float32
        ).astype(jnp.bfloat16)
        attended_grad_g = split_heads(attended_grad, heads_local)
        scores_again = (
            jnp.einsum("aqhe,akhe->ahqk", query, keyed, preferred_element_type=jnp.float32)
            * score_scale
        )
        probs_again = jnp.exp(scores_again - log_total)
        prob_grad = jnp.einsum(
            "aqhe,akhe->ahqk", attended_grad_g, valued, preferred_element_type=jnp.float32
        )
        value_grad = jnp.einsum(
            "ahqk,aqhe->akhe",
            probs_again.astype(jnp.bfloat16),
            attended_grad_g,
            preferred_element_type=jnp.float32,
        )
        score_grad = probs_again * (prob_grad - jnp.sum(probs_again * prob_grad, -1, keepdims=True))
        score_grad_low = score_grad.astype(jnp.bfloat16)
        query_grad = (
            jnp.einsum("ahqk,akhe->aqhe", score_grad_low, keyed, preferred_element_type=jnp.float32)
            * score_scale
        )
        key_grad = (
            jnp.einsum("ahqk,aqhe->akhe", score_grad_low, query, preferred_element_type=jnp.float32)
            * score_scale
        )
        proj_grad = jnp.stack(
            [join_heads(query_grad), join_heads(key_grad), join_heads(value_grad)]
        ).astype(jnp.bfloat16)
        grad_qkv = grad_qkv + jnp.einsum(
            "ld,tle->tde", conv_low, proj_grad, preferred_element_type=jnp.float32
        )
        conv_part = jnp.einsum(
            "tle,tde->ld", proj_grad, qkv_low, preferred_element_type=jnp.float32
        )
        conv_full = lax.psum(conv_part.astype(jnp.bfloat16), "mp").astype(jnp.float32)
        conv_pad = jnp.pad(conv_full, ((SIDE, SIDE), (0, 0)))
        grad_ext = lax.dynamic_slice_in_dim(conv_pad, begin, share + 2 * SIDE, 0)
        shifted_pad = jnp.pad(shifted, ((SIDE, SIDE), (0, 0)))
        shifted_ext = lax.dynamic_slice_in_dim(shifted_pad, begin_row * SIDE, share + 2 * SIDE, 0)
        shifted_share, kernel_attn_grad = conv_back_rows(
            grad_ext, shifted_ext, conv_attn, grid_rows
        )
        grad_conv_attn = grad_conv_attn + kernel_attn_grad
        normed_share = share_of(normed_one, begin, share)
        normed_first, first_back = jax.vjp(layer_norm, inputs_share)
        (input_norm_grad,) = first_back(shifted_share * (1.0 + scale_one))
        input_grads.append((resid_grad + input_norm_grad).astype(jnp.bfloat16))
        mod_parts.append(
            jnp.stack(
                [
                    jnp.sum(shifted_share, 0),
                    jnp.sum(shifted_share * normed_share, 0),
                    jnp.sum(attn_share * resid_grad, 0),
                    jnp.sum(mixed_grad, 0),
                    jnp.sum(mixed_grad * normed_two, 0),
                    jnp.sum(ffn_share * grad_share, 0),
                ]
            )
        )
    mod_total, conv_attn_total = (
        lax.psum(
            jnp.stack(mod_parts).reshape(slots, 6 * model_width).astype(jnp.bfloat16), "mp"
        ).astype(jnp.float32),
        lax.psum(grad_conv_attn.astype(jnp.bfloat16), "mp").astype(jnp.float32),
    )
    mod_full_grad = jnp.einsum(
        "sd,sc->dc",
        silu_cond.astype(jnp.float32),
        mod_total,
        precision=HIGHEST,
        preferred_element_type=jnp.float32,
    )
    mod_mean = (
        lax.psum_scatter(
            mod_full_grad.astype(jnp.bfloat16), "dp", scatter_dimension=0, tiled=True
        ).astype(jnp.float32)
        / dp_count
    )
    w_mod_new, mom_mod_new = momentum_update(w_mod, mom_mod, mod_mean, LEARN_RATE)
    merged_qkv = grad_qkv + err_qkv[0]
    merged_out = grad_out + err_out[0]
    merged_fc1 = grad_fc1 + err_fc1[0]
    merged_fc2 = grad_fc2 + err_fc2[0]
    left_qkv = jnp.einsum("tdo,tor->dr", merged_qkv, start_qkv, precision=HIGHEST)
    left_out = jnp.dot(merged_out, start_out, precision=HIGHEST)
    left_fc1 = jnp.dot(merged_fc1, start_fc1, precision=HIGHEST)
    left_fc2 = jnp.dot(merged_fc2, start_fc2, precision=HIGHEST)
    summed = (
        lax.psum(left_qkv.astype(jnp.bfloat16), "dp").astype(jnp.float32),
        lax.psum(left_out.astype(jnp.bfloat16), "dp").astype(jnp.float32),
        lax.psum(left_fc1.astype(jnp.bfloat16), "dp").astype(jnp.float32),
        lax.psum(left_fc2.astype(jnp.bfloat16), "dp").astype(jnp.float32),
        lax.psum(conv_attn_total.astype(jnp.bfloat16), "dp").astype(jnp.float32),
        lax.psum(grad_conv_ffn.astype(jnp.bfloat16), "dp").astype(jnp.float32),
    )
    basis_qkv = orthonormal(summed[0] / dp_count)
    basis_out = orthonormal(summed[1] / dp_count)
    basis_fc1 = orthonormal(summed[2] / dp_count)
    basis_fc2 = orthonormal(summed[3] / dp_count)
    conv_attn_new, mom_conv_attn_new = momentum_update(
        conv_attn, mom_conv_attn, summed[4] / dp_count, LEARN_RATE
    )
    conv_ffn_new, mom_conv_ffn_new = momentum_update(
        conv_ffn, mom_conv_ffn, summed[5] / dp_count, FAST_RATE
    )
    right_qkv = jnp.einsum("tdo,dr->tor", merged_qkv, basis_qkv, precision=HIGHEST)
    right_out = jnp.einsum("cd,cr->dr", merged_out, basis_out, precision=HIGHEST)
    right_fc1 = jnp.einsum("df,dr->fr", merged_fc1, basis_fc1, precision=HIGHEST)
    right_fc2 = jnp.einsum("fd,fr->dr", merged_fc2, basis_fc2, precision=HIGHEST)
    rights = (
        lax.psum(right_qkv.astype(jnp.bfloat16), "dp").astype(jnp.float32),
        lax.psum(right_out.astype(jnp.bfloat16), "dp").astype(jnp.float32),
        lax.psum(right_fc1.astype(jnp.bfloat16), "dp").astype(jnp.float32),
        lax.psum(right_fc2.astype(jnp.bfloat16), "dp").astype(jnp.float32),
    )
    approx_qkv = jnp.einsum("dr,tor->tdo", basis_qkv, rights[0] / dp_count, precision=HIGHEST)
    approx_out = jnp.einsum("cr,dr->cd", basis_out, rights[1] / dp_count, precision=HIGHEST)
    approx_fc1 = jnp.einsum("dr,fr->df", basis_fc1, rights[2] / dp_count, precision=HIGHEST)
    approx_fc2 = jnp.einsum("fr,dr->fd", basis_fc2, rights[3] / dp_count, precision=HIGHEST)
    w_qkv_new, mom_qkv_new = momentum_update(w_qkv, mom_qkv, approx_qkv, LEARN_RATE)
    w_out_new, mom_out_new = momentum_update(w_out, mom_out, approx_out, FAST_RATE)
    w_fc1_new, mom_fc1_new = momentum_update(w_fc1, mom_fc1, approx_fc1, LEARN_RATE)
    w_fc2_new, mom_fc2_new = momentum_update(w_fc2, mom_fc2, approx_fc2, LEARN_RATE)
    return (
        jnp.stack(outputs),
        jnp.stack(input_grads),
        w_mod_new,
        mom_mod_new,
        conv_attn_new,
        mom_conv_attn_new,
        w_qkv_new,
        mom_qkv_new,
        (merged_qkv - approx_qkv)[None],
        w_out_new,
        mom_out_new,
        (merged_out - approx_out)[None],
        w_fc1_new,
        mom_fc1_new,
        (merged_fc1 - approx_fc1)[None],
        conv_ffn_new,
        mom_conv_ffn_new,
        w_fc2_new,
        mom_fc2_new,
        (merged_fc2 - approx_fc2)[None],
    )


def solution(mesh):
    placed = (
        P("dp", "mp", None),
        P("dp", None),
        P("dp", "mp", None),
        P("dp"),
        P("dp", None),
        P("dp", None),
        P(),
        P(),
        P(None, None, "mp"),
        P(None, None, "mp"),
        P("dp", None, None, "mp"),
        P(None, "mp", None),
        P("mp", None),
        P("mp", None),
        P("dp", "mp", None),
        P(),
        P(None, "mp"),
        P(None, "mp"),
        P("dp", None, "mp"),
        P("mp", None),
        P(None, "mp"),
        P(None, "mp"),
        P("mp", None),
        P("mp", None),
        P("dp", "mp", None),
        P(),
    )
    return jax.shard_map(
        per_device,
        mesh=mesh,
        in_specs=placed,
        out_specs=(
            P("dp", "mp", None),
            P("dp", "mp", None),
            P("dp", None),
            P("dp", None),
            P(),
            P(),
            P(None, None, "mp"),
            P(None, None, "mp"),
            P("dp", None, None, "mp"),
            P("mp", None),
            P("mp", None),
            P("dp", "mp", None),
            P(None, "mp"),
            P(None, "mp"),
            P("dp", None, "mp"),
            P(None, "mp"),
            P(None, "mp"),
            P("mp", None),
            P("mp", None),
            P("dp", "mp", None),
        ),
        check_vma=False,
    )
```

profile of v0, /device:TPU:0, one launch (start us, length us, event | category | flops | bytes accessed | tf_op | source)
XLA Modules:
  0.0 1184.7 jit_solution(18165298556006606738)
XLA Ops:
  12.3 28.6 %all-gather.4.cloned.1.call-done = bf16[2,1024,768]{2,1,0:T(8,128)(2,1)} async-done(((bf16[2,256,768]{2,1,0:T(8,128)(2,1)}), bf16[2,1024,768]{2,1,0:T(8,128)(2,1)}) %all-gather.4.cloned.1.call-update) | async-done | bytes 3145744 | tf_op jit(solution)/shard_map/all_gather | solution.py:153
  50.8 101.7 %all-gather.6.cloned.1.call-done = bf16[768,4608]{1,0:T(8,128)(2,1)} async-done(((bf16[96,4608]{1,0:T(8,128)(2,1)}), bf16[768,4608]{1,0:T(8,128)(2,1)}) %all-gather.6.cloned.1.call-update) | async-done | bytes 7077904 | tf_op jit(solution)/shard_map/all_gather | solution.py:147
  152.5 4.0 fusion.256
  160.0 9.7 fusion.37
  211.6 62.9 %all-reduce.65.cloned.1.call-done = (bf16[1024,768]{1,0:T(8,128)(2,1)}, bf16[1024,768]{1,0:T(8,128)(2,1)}) async-done(((bf16[1024,768]{1,0:T(8,128)(2,1)}, bf16[1024,768]{1,0:T(8,128)(2,1)}), (bf16[1024,768]{1,0:T(8,128)(2,1)}, bf16[1024,768]{1,0:T(8,128)(2,1)})) %all-reduce.65.cloned.1.call-update) | async-done | bytes 3145744 | tf_op jit(solution)/shard_map/psum | solution.py:202
  274.6 8.2 multiply_add_fusion
  293.1 25.7 %fusion.19 = (bf16[32,32,768]{2,1,0:T(8,128)(2,1)}, f32[32,32,768]{2,1,0:T(8,128)}, bf16[32,32,768]{2,1,0:T(8,128)(2,1)}, f32[32,32,768]{2,1,0:T(8,128)}) fusion(f32[768]{0:T(1024)S(1)} %get-tuple-element.97, f32[768]{0:T(1024)S(1)} %get-tuple-element.90, f32[768]{0:T(1024)S(1)} %get-tuple-element.91, f32[768]{0:T(1024)S(1)} %get-tuple-element.92, ...), kind=kLoop, calls=%fused_computation.62 | loop fusion | flops 40894464 | bytes 15756288 | tf_op jit(solution)/shard_map/convert_element_type | solution.py:212
  318.9 18.4 %multiply_reduce_fusion.17 = (f32[768]{0:T(1024)S(1)}, f32[768]{0:T(1024)S(1)}, f32[768]{0:T(1024)S(1)}, f32[768]{0:T(1024)S(1)}, f32[768]{0:T(1024)S(1)}, /*ind...) fusion(f32[32,32,768]{2,1,0:T(8,128)} %bitcast.377, ...), kind=kOutput, calls=%fused_computation.158 | convolution fusion | flops 1238624256 | bytes 12217856 | tf_op jit(solution)/shard_map/ld,fd->lf/dot_general | solution.py:224
  337.3 9.2 multiply_reduce_fusion.8
  346.5 18.1 %broadcast_multiply_fusion = (f32[32,32,768]{2,1,0:T(8,128)}, f32[32,32,768]{2,1,0:T(8,128)}, f32[32,32,768]{2,1,0:T(8,128)}, f32[32,32,768]{2,1,0:T(8,128)}, f3...) fusion(f32[32,32,768]{2,1,0:T(8,128)} %bitcast.370, ...), kind=kLoop, calls=%fused_computation.240 | loop fusion | flops 14155776 | bytes 62942208 | tf_op jit(solution)/shard_map/transpose(jvp())/mul | solution.py:32
  364.6 6.1 pad_add_fusion
  370.7 6.4 fusion.62
  379.7 6.0 pad_add_fusion.1
  385.7 5.0 fusion.63
  397.4 5.3 convert_multiply_fusion.1
  431.1 5.2 fusion.205
  436.6 5.6 bitcast_add_fusion.5
  446.3 17.0 %all-reduce.63.cloned.1.call-done = (bf16[1024,768]{1,0:T(8,128)(2,1)}, bf16[1024,768]{1,0:T(8,128)(2,1)}) async-done(((bf16[1024,768]{1,0:T(8,128)(2,1)}, bf16[1024,768]{1,0:T(8,128)(2,1)}), (bf16[1024,768]{1,0:T(8,128)(2,1)}, bf16[1024,768]{1,0:T(8,128)(2,1)})) %all-reduce.63.cloned.1.call-update) | async-done | bytes 3145744 | tf_op jit(solution)/shard_map/psum | solution.py:238
  463.4 4.4 multiply_reduce_fusion.19
  471.1 3.9 bitcast_add_fusion.1
  607.6 37.6 %all-reduce.49 = (bf16[768,8]{0,1:T(8,128)(2,1)S(1)}, bf16[192,8]{0,1:T(8,128)(2,1)S(1)}, bf16[768,8]{0,1:T(8,128)(2,1)S(1)}, bf16[768,8]{0,1:T(8,128)(2,1)S(1)}) all-reduce(bf16[768,8]{0,1:T(8,128)(2,1)S(1)} %fusion.114, bf16[192,8]{0,1:T(8,128)(2,1)S(1)} %convolution_convert_fusion.19, ...), channel_id=1, replica_groups=mesh['dp'=8,'mp'=4] {'dp'}, use_global_device_ids=true, to_apply=%region_68.69 | all-reduce | flops 19968 | bytes 79872 | tf_op jit(solution)/shard_map/psum | solution.py:339
  649.3 5.3 multiply_reduce_fusion.150
  659.1 6.3 multiply_reduce_fusion.149
  666.1 3.8 multiply_reduce_fusion.148
  691.5 5.3 multiply_reduce_fusion.42
  701.2 6.4 multiply_reduce_fusion.41
  708.4 3.7 multiply_reduce_fusion.40
  715.3 5.0 multiply_reduce_fusion.39
  734.1 5.1 multiply_reduce_fusion.77
  743.5 6.2 multiply_reduce_fusion.76
  757.2 4.9 multiply_reduce_fusion.74
  772.5 5.2 multiply_reduce_fusion.112
  785.9 6.3 multiply_reduce_fusion.111
  799.9 4.8 multiply_reduce_fusion.109
  815.2 17.6 %subtract_multiply_fusion.23 = (f32[192,1]{0,1:T(1,128)S(1)}, f32[192,1]{0,1:T(1,128)S(1)}, f32[192,1]{0,1:T(1,128)S(1)}, f32[192,1]{0,1:T(1,128)S(1)}, f32[192,...) fusion(f32[192,1]{0,1:T(1,128)S(1)} %get-tuple-element.472, f32[]{:T(128)S(6)} %rsqrt.227, ...), kind=kLoop, calls=%fused_computation.780 | loop fusion | flops 12096 | bytes 11660 | tf_op jit(solution)/shard_map/mul | solution.py:96
  832.7 17.8 %subtract_multiply_fusion.2 = (f32[768,1]{0,1:T(1,128)S(1)}, f32[768,1]{0,1:T(1,128)S(1)}, f32[768,1]{0,1:T(1,128)S(1)}, f32[768,1]{0,1:T(1,128)S(1)}, f32[768,1...) fusion(f32[768,1]{0,1:T(1,128)S(1)} %get-tuple-element.297, f32[768,8]{0,1:T(8,128)S(1)} %convert_multiply_fusion.6, ...), kind=kLoop, calls=%fused_computation.703 | loop fusion | flops 48384 | bytes 46220 | tf_op jit(solution)/shard_map/mul | solution.py:96
  850.5 17.2 %subtract_multiply_fusion.9 = (f32[768,1]{0,1:T(1,128)S(1)}, f32[768,1]{0,1:T(1,128)S(1)}, f32[768,1]{0,1:T(1,128)S(1)}, f32[768,1]{0,1:T(1,128)S(1)}, f32[768,1...) fusion(f32[768,1]{0,1:T(1,128)S(1)} %get-tuple-element.326, f32[768,8]{0,1:T(8,128)S(1)} %convert_multiply_fusion.7, ...), kind=kLoop, calls=%fused_computation.711 | loop fusion | flops 48384 | bytes 46220 | tf_op jit(solution)/shard_map/mul | solution.py:96
  867.8 4.2 bitcast_convert_fusion.1
  875.0 17.7 %subtract_multiply_fusion.16 = (f32[768,1]{0,1:T(1,128)S(1)}, f32[768,1]{0,1:T(1,128)S(1)}, f32[768,1]{0,1:T(1,128)S(1)}, f32[768,1]{0,1:T(1,128)S(1)}, f32[768,...) fusion(f32[768,1]{0,1:T(1,128)S(1)} %get-tuple-element.385, f32[768,8]{0,1:T(8,128)S(1)} %convert_multiply_fusion.8, ...), kind=kLoop, calls=%fused_computation.719 | loop fusion | flops 48384 | bytes 46220 | tf_op jit(solution)/shard_map/mul | solution.py:96
  907.3 32.8 %all-reduce.61.cloned.1.call-done = (bf16[1024,768]{1,0:T(8,128)(2,1)}, bf16[1024,768]{1,0:T(8,128)(2,1)}) async-done(((bf16[1024,768]{1,0:T(8,128)(2,1)}, bf16[1024,768]{1,0:T(8,128)(2,1)}), (bf16[1024,768]{1,0:T(8,128)(2,1)}, bf16[1024,768]{1,0:T(8,128)(2,1)})) %all-reduce.61.cloned.1.call-update) | async-done | bytes 3145744 | tf_op jit(solution)/shard_map/psum | solution.py:285
  957.8 11.2 all-reduce.50
  969.3 5.0 convolution_convert_fusion
  978.4 62.8 %all-reduce.59.cloned.1.call-done = (bf16[9,768]{1,0:T(8,128)(2,1)}, bf16[3,192,8]{1,2,0:T(8,128)(2,1)}, bf16[768,8]{0,1:T(8,128)(2,1)}, bf16[768,8]{0,1:T(8,128...) async-done(((bf16[9,768]{1,0:T(8,128)(2,1)}, bf16[3,192,8]{1,2,0:T(8,128)(2,1)}, bf16[768,8]{0,1:T(8,128)(2,1)}, bf16[768,8]{0,1:T(8,128)(2,1)}, ...) | async-done | bytes 73744 | tf_op jit(solution)/shard_map/psum | solution.py:343
  1047.4 4.4 multiply_subtract_fusion.2
  1051.9 5.6 multiply_subtract_fusion.1
  1057.6 5.6 multiply_subtract_fusion
  1063.2 110.1 %reduce-scatter.8.cloned.1.call-done = bf16[96,4608]{1,0:T(8,128)(2,1)} async-done(((bf16[768,4608]{1,0:T(8,128)(2,1)}), bf16[96,4608]{1,0:T(8,128)(2,1)}) %reduce-scatter.8.cloned.1.call-update) | async-done | bytes 884752 | tf_op jit(solution)/shard_map/reduce_scatter | solution.py:324
  1173.3 4.1 multiply_subtract_fusion.3
  (681 shorter events, 371.3 us)
Async XLA Ops:
  7.2 418.3 %copy-start = (f32[768,8]{0,1:T(8,128)S(1)}, f32[768,8]{0,1:T(8,128)}, u32[]{:S(2)}) copy-start(f32[768,8]{0,1:T(8,128)} %param.51) | copy-start | bytes 73732
  7.2 33.7 %all-gather.4.cloned.1.call-start = ((), (), s32[]{:S(2)}) async-start(), calls=%async_computation.3 | async-start | bytes 3932160 | tf_op jit(solution)/shard_map/all_gather | solution.py:153
  8.0 144.5 %all-gather.6.cloned.1.call-start = ((), (), s32[]{:S(2)}) async-start(), calls=%async_computation.4 | async-start | bytes 7962624 | tf_op jit(solution)/shard_map/all_gather | solution.py:147
  10.5 264.0 %all-reduce.65.cloned.1.call-start = ((), (), s32[]{:S(2)}) async-start(), calls=%async_computation.12 | async-start | bytes 6291456 | tf_op jit(solution)/shard_map/psum | solution.py:202
  10.6 194.0 %copy-start.43 = (bf16[192,768]{1,0:T(8,128)(2,1)}, bf16[192,768]{1,0:T(8,128)(2,1)S(1)}, u32[]{:S(2)}) copy-start(bf16[192,768]{1,0:T(8,128)(2,1)S(1)} %convert_element_type.363) | copy-start | bytes 884740
  44.1 6.7 copy-start.119
  47.6 104.9 %copy-start.150 = (bf16[2,768]{1,0:T(2,128)(2,1)S(1)}, bf16[2,768]{1,0:T(2,128)(2,1)}, u32[]{:S(2)}) copy-start(bf16[2,768]{1,0:T(2,128)(2,1)} %param.27) | copy-start | bytes 9220
  50.8 106.5 %copy-start.31 = (f32[1,1024,768]{2,1,0:T(8,128)S(1)}, f32[1,1024,768]{2,1,0:T(8,128)}, u32[]{:S(2)}) copy-start(f32[1,1024,768]{2,1,0:T(8,128)} %get-tuple-element.432) | copy-start | bytes 9437188
  157.2 117.3 %copy-start.107 = (f32[768]{0:T(1024)}, f32[768]{0:T(1024)S(1)}, u32[]{:S(2)}) copy-start(f32[768]{0:T(1024)S(1)} %get-tuple-element.87) | copy-start | bytes 9220
  157.2 117.3 %copy-start.109 = (f32[768]{0:T(1024)}, f32[768]{0:T(1024)S(1)}, u32[]{:S(2)}) copy-start(f32[768]{0:T(1024)S(1)} %get-tuple-element.82) | copy-start | bytes 9220
  157.2 117.3 %copy-start.117 = (f32[768]{0:T(1024)}, f32[768]{0:T(1024)S(1)}, u32[]{:S(2)}) copy-start(f32[768]{0:T(1024)S(1)} %get-tuple-element.83) | copy-start | bytes 9220
  174.2 22.4 %copy-start.58 = (bf16[4,256,3,64]{1,3,2,0:T(8,128)(2,1)}, bf16[4,256,3,64]{1,3,2,0:T(8,128)(2,1)S(1)}, u32[]{:S(2)}) copy-start(bf16[4,256,3,64]{1,3,2,0:T(8,128)(2,1)S(1)} %copy.87) | copy-start | bytes 1179652
  175.6 21.0 %copy-start.60 = (bf16[4,256,3,64]{1,3,2,0:T(8,128)(2,1)}, bf16[4,256,3,64]{1,3,2,0:T(8,128)(2,1)S(1)}, u32[]{:S(2)}) copy-start(bf16[4,256,3,64]{1,3,2,0:T(8,128)(2,1)S(1)} %copy.86) | copy-start | bytes 1179652
  177.0 20.9 %copy-start.62 = (bf16[4,256,3,64]{1,3,2,0:T(8,128)(2,1)}, bf16[4,256,3,64]{1,3,2,0:T(8,128)(2,1)S(1)}, u32[]{:S(2)}) copy-start(bf16[4,256,3,64]{1,3,2,0:T(8,128)(2,1)S(1)} %copy.88) | copy-start | bytes 1179652
  182.5 8.8 copy-start.64
  185.2 6.7 copy-start.66
  207.6 111.3 %all-gather.8.cloned.1.call-start = ((), (), s32[]{:S(2)}) async-start(), calls=%async_computation.7 | async-start | bytes 3932160 | tf_op jit(solution)/shard_map/all_gather | solution.py:154
  208.1 255.2 %all-reduce.63.cloned.1.call-start = ((), (), s32[]{:S(2)}) async-start(), calls=%async_computation.11 | async-start | bytes 6291456 | tf_op jit(solution)/shard_map/psum | solution.py:238
  209.3 65.3 %copy-start.120 = (f32[1024]{0:T(1024)S(1)}, f32[1024]{0:T(1024)}, u32[]{:S(2)}) copy-start(f32[1024]{0:T(1024)} %copy-done.119) | copy-start | bytes 12292
  209.3 65.3 %copy-start.140 = (f32[768]{0:T(1024)S(1)}, f32[768]{0:T(1024)}, u32[]{:S(2)}) copy-start(f32[768]{0:T(1024)} %copy-done.139) | copy-start | bytes 9220
  209.3 65.3 %copy-start.142 = (f32[768]{0:T(1024)S(1)}, f32[768]{0:T(1024)}, u32[]{:S(2)}) copy-start(f32[768]{0:T(1024)} %copy-done.141) | copy-start | bytes 9220
  209.3 65.3 %copy-start.144 = (f32[1024]{0:T(1024)S(1)}, f32[1024]{0:T(1024)}, u32[]{:S(2)}) copy-start(f32[1024]{0:T(1024)} %copy-done.143) | copy-start | bytes 12292
  209.3 65.3 %copy-start.146 = (f32[1024]{0:T(1024)S(1)}, f32[1024]{0:T(1024)}, u32[]{:S(2)}) copy-start(f32[1024]{0:T(1024)} %copy-done.145) | copy-start | bytes 12292
  293.1 25.8 %copy-start.153 = (f32[768]{0:T(1024)S(1)}, f32[768]{0:T(1024)}, u32[]{:S(2)}) copy-start(f32[768]{0:T(1024)} %get-tuple-element.77) | copy-start | bytes 9220
  318.9 18.4 %copy-start.27 = (f32[32,32,768]{2,1,0:T(8,128)S(1)}, f32[32,32,768]{2,1,0:T(8,128)}, u32[]{:S(2)}) copy-start(f32[32,32,768]{2,1,0:T(8,128)} %get-tuple-element.468) | copy-start | bytes 9437188
  318.9 18.4 %copy-start.32 = (bf16[2,1024,768]{2,1,0:T(8,128)(2,1)S(1)}, bf16[2,1024,768]{2,1,0:T(8,128)(2,1)}, u32[]{:S(2)}) copy-start(bf16[2,1024,768]{2,1,0:T(8,128)(2,1)} %all-gather.8.cloned.1.call-done) | copy-start | bytes 9437188
  318.9 18.4 %copy-start.35 = (f32[1024,768]{1,0:T(8,128)S(1)}, f32[1024,768]{1,0:T(8,128)}, u32[]{:S(2)}) copy-start(f32[1024,768]{1,0:T(8,128)} %fusion.207) | copy-start | bytes 9437188
  318.9 18.4 %copy-start.152 = (f32[768]{0:T(1024)S(1)}, f32[768]{0:T(1024)}, u32[]{:S(2)}) copy-start(f32[768]{0:T(1024)} %get-tuple-element.80) | copy-start | bytes 9220
  394.4 508.2 %reduce-scatter.4.cloned.1.call-start = ((), (), s32[]{:S(2)}) async-start(), calls=%async_computation.5 | async-start | bytes 1966080 | tf_op jit(solution)/shard_map/reduce_scatter | solution.py:214
  394.9 7.9 copy-start.155
  394.9 7.8 copy-start.157
  406.6 498.5 %reduce-scatter.6.cloned.1.call-start = ((), (), s32[]{:S(2)}) async-start(), calls=%async_computation.6 | async-start | bytes 1966080 | tf_op jit(solution)/shard_map/reduce_scatter | solution.py:214
  436.3 7.2 copy-start.147
  436.4 503.8 %all-reduce.61.cloned.1.call-start = ((), (), s32[]{:S(2)}) async-start(), calls=%async_computation.10 | async-start | bytes 6291456 | tf_op jit(solution)/shard_map/psum | solution.py:285
  481.9 11.3 copy-start.103
  502.7 11.8 copy-start.101
  874.6 166.6 %all-reduce.59.cloned.1.call-start = ((), (), s32[]{:S(2)}) async-start(), calls=%async_computation.9 | async-start | bytes 196608 | tf_op jit(solution)/shard_map/psum | solution.py:343
  892.8 7.8 copy-start.22
  895.1 7.5 copy-start.154
  907.3 34.4 %copy-start.57 = (f32[320,768]{1,0:T(8,128)S(1)}, f32[320,768]{1,0:T(8,128)}, u32[]{:S(2)}) copy-start(f32[320,768]{1,0:T(8,128)} %get-tuple-element.501) | copy-start | bytes 2949124
  954.3 14.9 %copy-start.151 = (bf16[2,768]{1,0:T(2,128)(2,1)S(1)}, bf16[2,768]{1,0:T(2,128)(2,1)}, u32[]{:S(2)}) copy-start(bf16[2,768]{1,0:T(2,128)(2,1)} %param.27) | copy-start | bytes 9220
  968.9 204.4 %reduce-scatter.8.cloned.1.call-start = ((), (), s32[]{:S(2)}) async-start(), calls=%async_computation.8 | async-start | bytes 7962624 | tf_op jit(solution)/shard_map/reduce_scatter | solution.py:324
  974.3 66.9 %copy-start.112 = (f32[9,768]{1,0:T(8,128)S(1)}, f32[9,768]{1,0:T(8,128)}, u32[]{:S(2)}) copy-start(f32[9,768]{1,0:T(8,128)} %param.32) | copy-start | bytes 82948
  974.3 68.5 %copy-start.114 = (f32[9,768]{1,0:T(8,128)S(1)}, f32[9,768]{1,0:T(8,128)}, u32[]{:S(2)}) copy-start(f32[9,768]{1,0:T(8,128)} %param.46) | copy-start | bytes 82948
  974.3 70.0 %copy-start.38 = (f32[192,768]{1,0:T(8,128)S(1)}, f32[192,768]{1,0:T(8,128)}, u32[]{:S(2)}) copy-start(f32[192,768]{1,0:T(8,128)} %copy-done.37) | copy-start | bytes 1769476
  974.3 70.0 %copy-start.74 = (f32[192,768]{1,0:T(8,128)S(1)}, f32[192,768]{1,0:T(8,128)}, u32[]{:S(2)}) copy-start(f32[192,768]{1,0:T(8,128)} %param.38) | copy-start | bytes 1769476
  976.3 71.1 %copy-start.11 = (f32[3,768,192]{1,2,0:T(8,128)S(1)}, f32[3,768,192]{1,2,0:T(8,128)}, u32[]{:S(2)}) copy-start(f32[3,768,192]{1,2,0:T(8,128)} %copy-done.10) | copy-start | bytes 5308420
  1057.6 115.7 %copy-start.47 = (f32[96,4608]{1,0:T(8,128)S(1)}, f32[96,4608]{1,0:T(8,128)}, u32[]{:S(2)}) copy-start(f32[96,4608]{1,0:T(8,128)} %param.30) | copy-start | bytes 5308420
  (127 other events, 360.0 us)
Sparse Core Ops, SparseCore 0:
  9.6 31.2 all-gather.3
  43.7 108.7 all-gather.5
  207.7 66.8 all-reduce.64
  276.0 28.6 all-gather.7
  394.5 68.7 all-reduce.62
  466.3 28.2 reduce-scatter.3
  497.9 28.1 reduce-scatter.5
  874.8 65.3 all-reduce.60
  969.1 72.0 all-reduce.58
  1044.7 128.5 reduce-scatter.7
where the time goes:
time: 1200 us; the launch traced here: 1180 us
  waiting for transfers between devices  417 us (35%)
  other arithmetic  388 us (32%)
  local copies, waits for them, and re-layouts  145 us (12%)
  matrix products  144 us (12%)
  blocking collectives  48.7 us (4%)
  between operations  40.1 us (3%)
    reduce_sum x37, other arithmetic, orthonormal(): current = current - jnp.sum(earlier * current, -1, keepdims=True) * earlier  112 us
    reduce_scatter x1, waiting for transfers between devices, per_device(): lax.psum_scatter(mod_full_grad.astype(jnp.bfloat16), 'dp', scatter_dimens...  110 us
    all_gather x1, waiting for transfers between devices, per_device(): lax.all_gather(w_mod.astype(jnp.bfloat16), 'dp', axis=0, tiled=True)  102 us
    mul x7, other arithmetic, orthonormal(): current * lax.rsqrt(jnp.sum(current * current, -1, keepdims=True) + ORTHO...  70.3 us
    psum x1, waiting for transfers between devices, per_device(): lax.psum(attn_part.astype(jnp.bfloat16), 'mp').astype(jnp.float32)  62.9 us
    psum x1, waiting for transfers between devices, per_device(): lax.psum(conv_attn_total.astype(jnp.bfloat16), 'dp').astype(jnp.float32)  62.8 us
    psum x1, blocking collectives, per_device(): lax.psum(left_qkv.astype(jnp.bfloat16), 'dp').astype(jnp.float32)  37.6 us
    reduce_sum x20, other arithmetic, orthonormal(): jnp.sum(current * current, -1, keepdims=True) + ORTHO_EPS  33.3 us
  transfers between devices with their start and end apart: 10, of which 7 were waited for; matrix products, arithmetic and copies ran while one was open for 43% of the time, Pallas kernels for 0%

commit v1 on v0

v1 whole, which is shorter than its diff:
```python
import functools

import jax
import jax.numpy as jnp
from jax import lax
from jax.experimental import pallas as pl
from jax.experimental.pallas import tpu as pltpu
from jax.sharding import PartitionSpec as P

HEAD_DIM = 64
SIDE = 32
HALF = SIDE // 2
PHASE = HALF * HALF
TOKENS = SIDE * SIDE
PADDED = PHASE + 2 * HALF
LANES = 256
ROWS = 32

NORM_EPS = 1e-06
ORTHO_EPS = 1e-06
LEARN_RATE = 0.005
FAST_RATE = 0.025
MOMENTUM = 0.9
HIGHEST = lax.Precision.HIGHEST
GELU_C = 0.7978845608
GELU_A = 0.044715

f32 = jnp.float32
bf16 = jnp.bfloat16
VMEM = pl.BlockSpec(memory_space=pltpu.VMEM)
SMEM = pl.BlockSpec(memory_space=pltpu.SMEM)


def params(mib, **more):
    return pltpu.CompilerParams(vmem_limit_bytes=mib << 20, **more)


def cost(flops, nbytes, trans=0):
    return pl.CostEstimate(flops=flops, bytes_accessed=nbytes, transcendentals=trans)


def dot_nn(a, b):
    return lax.dot_general(a, b, (((1,), (0,)), ((), ())), preferred_element_type=f32)


def dot_nt(a, b):
    return lax.dot_general(a, b, (((1,), (1,)), ((), ())), preferred_element_type=f32)


def dot_tn(a, b):
    return lax.dot_general(a, b, (((0,), (0,)), ((), ())), preferred_element_type=f32)


def taps_of(a, b):
    rows = (((1, -1), (0, 0), (1, 0)) if a == 0 else ((0, 0), (1, 0), (0, 1)))
    cols = (((1, True), (0, False), (1, False)) if b == 0 else ((0, False), (1, False), (0, True)))
    return [
        (3 * i + j, 2 * rows[i][0] + cols[j][0], cols[j][1], rows[i][1])
        for i in range(3)
        for j in range(3)
    ]


TAPS = [taps_of(g // 2, g % 2) for g in range(4)]


def shift_columns(values, phase):
    place = lax.broadcasted_iota(jnp.int32, values.shape, 0)
    if phase % 2 == 1:
        return jnp.where(place == 0, 0.0, pltpu.roll(values, 1, 0))
    return jnp.where(place == HALF - 1, 0.0, pltpu.roll(values, HALF - 1, 0))


def zero_edges(*buffers):
    for buffer in buffers:
        lanes = buffer.shape[-1]
        for g in range(4):
            buffer[g, 0:HALF, :] = jnp.zeros((HALF, lanes), f32)
            buffer[g, HALF + PHASE : PADDED, :] = jnp.zeros((HALF, lanes), f32)


def tap_rows(plain, shifted, g, tap, row, lanes):
    _, phase, moved, step = TAPS[g][tap]
    buffer = shifted if moved else plain
    start = pl.multiple_of(HALF + (row + step) * HALF, HALF)
    return buffer[phase, pl.ds(start, HALF), lanes]


def spread_kernel(k_ref, lanes, flip):
    width = lanes.stop - lanes.start
    return [
        jnp.broadcast_to(k_ref[(8 - t if flip else t) : (8 - t if flip else t) + 1, lanes], (8, width))
        for t in range(9)
    ]


def conv_row(plain, shifted, spread, g, row, lanes):
    width = lanes.stop - lanes.start
    total = None
    for t in range(9):
        value = tap_rows(plain, shifted, g, t, row, lanes).reshape(2, 8, width)
        term = spread[t][None] * value
        total = term if total is None else total + term
    return total.reshape(HALF, width)


def kernel_sums(plain, shifted, grads, lanes):
    width = lanes.stop - lanes.start

    def body(row, sums):
        sums = list(sums)
        for g in range(4):
            start = pl.multiple_of(HALF + row * HALF, HALF)
            grad = grads[g, pl.ds(start, HALF), lanes].reshape(2, 8, width)
            for t in range(9):
                value = tap_rows(plain, shifted, g, t, row, lanes).reshape(2, 8, width)
                term = value * grad
                sums[t] = sums[t] + (term[0] + term[1])
        return tuple(sums)

    return lax.fori_loop(0, HALF, body, tuple(jnp.zeros((8, width), f32) for _ in range(9)))


def grid_permutation(inverse):
    size = 8 * SIDE
    token = lax.broadcasted_iota(jnp.int32, (size, size), 0 if inverse else 1)
    place = lax.broadcasted_iota(jnp.int32, (size, size), 1 if inverse else 0)
    r, c = token >> 5, token & 31
    target = ((r & 1) * 2 + (c & 1)) * 64 + (r >> 1) * HALF + (c >> 1)
    return jnp.where(target == place, 1.0, 0.0).astype(bf16)


def enter_kernel(slot_ref, lat_ref, cot_ref, own_l, own_c, snd_l, snd_c):
    perm = grid_permutation(False)
    mine = slot_ref[0]
    other = 1 - mine
    own_l[...] = dot_nn(perm, lat_ref[mine]).astype(bf16)
    snd_l[...] = dot_nn(perm, lat_ref[other]).astype(bf16)
    own_c[...] = dot_nn(perm, cot_ref[mine]).astype(bf16)
    snd_c[...] = dot_nn(perm, cot_ref[other]).astype(bf16)


def enter(slot, latents, cotangent):
    share, width = latents.shape[1:]
    piece = jax.ShapeDtypeStruct((share, width), bf16)
    return pl.pallas_call(
        enter_kernel,
        out_shape=(piece,) * 4,
        in_specs=[SMEM, VMEM, VMEM],
        out_specs=(VMEM,) * 4,
        compiler_params=params(24),
        cost_estimate=cost(4 * 2 * share * share * width, 12 * share * width),
        name="enter",
    )(slot, latents, cotangent)


def pack_attn_kernel(qkv_ref, out_ref, packed):
    local = qkv_ref.shape[2]
    row = lax.broadcasted_iota(jnp.int32, (local, local), 0)
    col = lax.broadcasted_iota(jnp.int32, (local, local), 1)
    eye = jnp.where(row == col, 1.0, 0.0).astype(bf16)
    for t in range(3):
        packed[t * local : (t + 1) * local, :] = dot_nt(eye, qkv_ref[t].astype(bf16)).astype(bf16)
    packed[3 * local : 4 * local, :] = out_ref[...].astype(bf16)


def pack_attn(w_qkv, w_out):
    local, width = w_out.shape
    return pl.pallas_call(
        pack_attn_kernel,
        out_shape=jax.ShapeDtypeStruct((4 * local, width), bf16),
        in_specs=[VMEM, VMEM],
        out_specs=VMEM,
        compiler_params=params(24),
        cost_estimate=cost(6 * local * local * width, 24 * local * width),
        name="pack_attn",
    )(w_qkv, w_out)


def norm_rows(values):
    mean = jnp.mean(values, -1, keepdims=True)
    centred = values - mean
    variance = jnp.mean(centred * centred, -1, keepdims=True)
    scale = lax.rsqrt(variance + NORM_EPS)
    return centred * scale, scale


def place_pieces(midx_ref, pieces, whole):
    for i, piece in enumerate(pieces):
        block = midx_ref[i]
        for g in range(4):
            start = pl.multiple_of(g * PHASE + block * 64, 64)
            whole[pl.ds(start, 64), :] = piece[g * 64 : (g + 1) * 64, :]


def fill_shifted(lat_ref, mod_ref, plain, shifted):
    gain = 1.0 + mod_ref[1:2, :]
    bias = mod_ref[0:1, :]
    for g in range(4):

        def body(j, carry):
            values = lat_ref[pl.ds(pl.multiple_of(g * PHASE + j * ROWS, ROWS), ROWS), :].astype(f32)
            normed, _ = norm_rows(values)
            result = normed * gain + bias
            start = pl.multiple_of(HALF + j * ROWS, HALF)
            plain[g, pl.ds(start, ROWS), :] = result
            for h in range(ROWS // HALF):
                part = result[h * HALF : (h + 1) * HALF]
                shifted[g, pl.ds(start + h * HALF, HALF), :] = shift_columns(part, g)
            return carry

        lax.fori_loop(0, PHASE // ROWS, body, 0)


def first_conv_kernel(midx_ref, p0, p1, p2, p3, mod_ref, k_ref, lat_ref, conv_ref, plain, shifted):
    place_pieces(midx_ref, (p0, p1, p2, p3), lat_ref)
    zero_edges(plain, shifted)
    fill_shifted(lat_ref, mod_ref, plain, shifted)
    for first in range(0, conv_ref.shape[1], LANES):
        lanes = slice(first, first + LANES)
        spread = spread_kernel(k_ref, lanes, False)
        for g in range(4):

            def body(row, carry):
                result = conv_row(plain, shifted, spread, g, row, lanes)
                start = pl.multiple_of(g * PHASE + row * HALF, HALF)
                conv_ref[pl.ds(start, HALF), lanes] = result.astype(bf16)
                return carry

            lax.fori_loop(0, HALF, body, 0)


def first_conv(midx, pieces, mod, kernel):
    width = pieces[0].shape[1]
    whole = jax.ShapeDtypeStruct((TOKENS, width), bf16)
    return pl.pallas_call(
        first_conv_kernel,
        out_shape=(whole, whole),
        in_specs=[SMEM] + [VMEM] * 6,
        out_specs=(VMEM, VMEM),
        scratch_shapes=[pltpu.VMEM((4, PADDED, width), f32)] * 2,
        compiler_params=params(32),
        cost_estimate=cost(30 * TOKENS * width, 6 * TOKENS * width),
        name="first_conv",
    )(midx, *pieces, mod, kernel)


def head_mask(shape, half):
    lane = lax.broadcasted_iota(jnp.int32, shape, 1)
    return (lane < HEAD_DIM) if half == 0 else (lane >= HEAD_DIM)


def attn_forward_kernel(conv_ref, wa_ref, wb_ref, wcat, proj_ref, att_t_ref, lse_ref, part_ref):
    local = wa_ref.shape[0] // 4
    both = 2 * local

    @pl.when(pl.program_id(0) == 0)
    def _():
        for t in range(4):
            wcat[t * both : t * both + local, :] = wa_ref[t * local : (t + 1) * local, :]
            wcat[t * both + local : (t + 1) * both, :] = wb_ref[t * local : (t + 1) * local, :]

    proj_ref[...] = dot_nt(conv_ref[...], wcat[0 : 3 * both, :]).astype(bf16)
    for pair in range(both // 128):
        q = proj_ref[:, pair * 128 : (pair + 1) * 128] * jnp.asarray(HEAD_DIM**-0.5, bf16)
        k = proj_ref[:, both + pair * 128 : both + (pair + 1) * 128]
        v = proj_ref[:, 2 * both + pair * 128 : 2 * both + (pair + 1) * 128]
        v_t = v.T
        for half in range(2):
            q_half = jnp.where(head_mask(q.shape, half), q, jnp.zeros_like(q))
            scores = dot_nt(k, q_half)
            top = jnp.max(scores, 0, keepdims=True)
            weights = jnp.exp(scores - top)
            total = jnp.sum(weights, 0, keepdims=True)
            probs = (weights * (1.0 / total)).astype(bf16)
            head = 2 * pair + half
            lse_ref[head : head + 1, :] = top + jnp.log(total)
            out_t = dot_nn(v_t[half * HEAD_DIM : (half + 1) * HEAD_DIM, :], probs)
            att_t_ref[head * HEAD_DIM : (head + 1) * HEAD_DIM, :] = out_t.astype(bf16)
    part_ref[...] = dot_tn(att_t_ref[...], wcat[3 * both : 4 * both, :]).astype(bf16)


def attn_forward(conv_low, wa, wb):
    rows, width = wa.shape
    both = rows // 2
    block = lambda g: (g, 0)
    fixed = lambda g: (0, 0)
    return pl.pallas_call(
        attn_forward_kernel,
        grid=(4,),
        out_shape=(
            jax.ShapeDtypeStruct((2 * rows, width), bf16),
            jax.ShapeDtypeStruct((TOKENS, 3 * both), bf16),
            jax.ShapeDtypeStruct((4, both, PHASE), bf16),
            jax.ShapeDtypeStruct((4, 8, PHASE), f32),
            jax.ShapeDtypeStruct((TOKENS, width), bf16),
        ),
        in_specs=[
            pl.BlockSpec((PHASE, width), block),
            pl.BlockSpec((rows, width), fixed),
            pl.BlockSpec((rows, width), fixed),
        ],
        out_specs=(
            pl.BlockSpec((2 * rows, width), fixed),
            pl.BlockSpec((PHASE, 3 * both), block),
            pl.BlockSpec((None, both, PHASE), lambda g: (g, 0, 0)),
            pl.BlockSpec((None, 8, PHASE), lambda g: (g, 0, 0)),
            pl.BlockSpec((PHASE, width), block),
        ),
        compiler_params=params(48),
        cost_estimate=cost(8 * TOKENS * both * width + 8 * TOKENS * PHASE * both, 16 << 20),
        name="attn_forward",
    )(conv_low, wa, wb)


def second_norm_kernel(midx_ref, lat_ref, po_ref, pr_ref, c0, c1, c2, c3, mod_ref, mixed, mixed_t, fgl, cot):
    place_pieces(midx_ref, (c0, c1, c2, c3), cot)
    gate_one = mod_ref[2:3, :]
    bias = mod_ref[3:4, :]
    gain = 1.0 + mod_ref[4:5, :]
    gate_two = mod_ref[5:6, :]
    live = mod_ref[6:7, :]

    def body(j, carry):
        rows = pl.ds(pl.multiple_of(j * ROWS, ROWS), ROWS)
        attn = po_ref[rows, :].astype(f32) + pr_ref[rows, :].astype(f32)
        resid = lat_ref[rows, :].astype(f32) + gate_one * attn
        normed, _ = norm_rows(resid)
        mixed[rows, :] = (normed * gain + bias).astype(bf16)
        grad = live * cot[rows, :].astype(f32)
        cot[rows, :] = grad.astype(bf16)
        fgl[rows, :] = (gate_two * grad).astype(bf16)
        return carry

    lax.fori_loop(0, TOKENS // ROWS, body, 0)
    mixed_t[...] = mixed[...].T


def second_norm(midx, lat, own, got, cots, mod):
    width = lat.shape[1]
    whole = jax.ShapeDtypeStruct((TOKENS, width), bf16)
    return pl.pallas_call(
        second_norm_kernel,
        out_shape=(whole, jax.ShapeDtypeStruct((width, TOKENS), bf16), whole, whole),
        in_specs=[SMEM] + [VMEM] * 8,
        out_specs=(VMEM,) * 4,
        compiler_params=params(32),
        cost_estimate=cost(20 * TOKENS * width, 16 * TOKENS * width),
        name="second_norm",
    )(midx, lat, own, got, *cots, mod)


def ffn_kernel(first, mixed, mixed_t, fgl, w1_ref, w2_ref, k_ref, *rest):
    if first:
        ffn_out, mix_out, g1_ref, g2_ref, kg_ref = rest[:5]
        scratch = rest[5:]
    else:
        ffn_in, mix_in, ffn_out, mix_out, g1_ref, g2_ref, kg_ref = rest[:7]
        scratch = rest[7:]
    plain, shifted, grad, grad_shifted, act, hidden_grad, ffn_acc, mix_acc = scratch
    step = pl.program_id(0)
    lanes = slice(0, w1_ref.shape[1])

    @pl.when(step == 0)
    def _():
        zero_edges(plain, shifted, grad, grad_shifted)
        if first:
            ffn_acc[...] = jnp.zeros_like(ffn_acc)
            mix_acc[...] = jnp.zeros_like(mix_acc)
        else:
            ffn_acc[...] = ffn_in[...].astype(f32)
            mix_acc[...] = mix_in[...].astype(f32)

    for g in range(4):
        rows = slice(g * PHASE, (g + 1) * PHASE)
        plain[g, HALF : HALF + PHASE, :] = dot_nn(mixed[rows, :], w1_ref[...])
        grad[g, HALF : HALF + PHASE, :] = dot_nt(fgl[rows, :], w2_ref[...])
    for g in range(4):

        def shift_body(row, carry):
            rows = pl.ds(pl.multiple_of(HALF + row * HALF, HALF), HALF)
            shifted[g, rows, :] = shift_columns(plain[g, rows, :], g)
            return carry

        lax.fori_loop(0, HALF, shift_body, 0)
    spread = spread_kernel(k_ref, lanes, False)
    for g in range(4):

        def act_body(row, carry):
            pre = conv_row(plain, shifted, spread, g, row, lanes)
            square = pre * pre
            tanh = jnp.tanh(pre * (GELU_C + (GELU_C * GELU_A) * square))
            half = 0.5 + 0.5 * tanh
            rows = pl.ds(pl.multiple_of(g * PHASE + row * HALF, HALF), HALF)
            act[rows, :] = (pre * half).astype(bf16)
            slope = half + (0.5 * pre) * (1.0 - tanh * tanh) * (
                GELU_C + (3.0 * GELU_C * GELU_A) * square
            )
            padded = pl.ds(pl.multiple_of(HALF + row * HALF, HALF), HALF)
            result = grad[g, padded, :] * slope
            grad[g, padded, :] = result
            grad_shifted[g, padded, :] = shift_columns(result, g)
            return carry

        lax.fori_loop(0, HALF, act_body, 0)
    flipped = spread_kernel(k_ref, lanes, True)
    for g in range(4):

        def back_body(row, carry):
            result = conv_row(grad, grad_shifted, flipped, g, row, lanes)
            rows = pl.ds(pl.multiple_of(g * PHASE + row * HALF, HALF), HALF)
            hidden_grad[rows, :] = result.astype(bf16)
            return carry

        lax.fori_loop(0, HALF, back_body, 0)
    sums = kernel_sums(plain, shifted, grad, lanes)
    for t in range(9):
        kg_ref[t : t + 1, :] = jnp.sum(sums[t], 0, keepdims=True)
    g2_ref[...] = dot_tn(act[...], fgl[...]).astype(g2_ref.dtype)
    g1_ref[...] = dot_nn(mixed_t[...], hidden_grad[...]).astype(g1_ref.dtype)
    for g in range(4):
        rows = slice(g * PHASE, (g + 1) * PHASE)
        ffn_acc[rows, :] += dot_nn(act[rows, :], w2_ref[...])
        mix_acc[rows, :] += dot_nt(hidden_grad[rows, :], w1_ref[...])

    @pl.when(step == pl.num_programs(0) - 1)
    def _():
        ffn_out[...] = ffn_acc[...].astype(ffn_out.dtype)
        mix_out[...] = mix_acc[...].astype(mix_out.dtype)


def ffn(mixed, mixed_t, fgl, w1, w2, kernel, before, grad_type):
    width, units = w1.shape
    first = before is None
    fixed = lambda i: (0, 0)
    whole = pl.BlockSpec((TOKENS, width), fixed)
    part_type = f32 if first else bf16
    padded = pltpu.VMEM((4, PADDED, LANES), f32)
    in_specs = [
        whole,
        pl.BlockSpec((width, TOKENS), fixed),
        whole,
        pl.BlockSpec((width, LANES), lambda i: (0, i)),
        pl.BlockSpec((LANES, width), lambda i: (i, 0)),
        pl.BlockSpec((9, LANES), lambda i: (0, i)),
    ]
    operands = [mixed, mixed_t, fgl, w1, w2, kernel]
    if not first:
        in_specs += [whole, whole]
        operands += list(before)
    return pl.pallas_call(
        functools.partial(ffn_kernel, first),
        grid=(units // LANES,),
        out_shape=(
            jax.ShapeDtypeStruct((TOKENS, width), part_type),
            jax.ShapeDtypeStruct((TOKENS, width), part_type),
            jax.ShapeDtypeStruct((width, units), grad_type),
            jax.ShapeDtypeStruct((units, width), grad_type),
            jax.ShapeDtypeStruct((9, units), f32),
        ),
        in_specs=in_specs,
        out_specs=(
            whole,
            whole,
            pl.BlockSpec((width, LANES), lambda i: (0, i)),
            pl.BlockSpec((LANES, width), lambda i: (i, 0)),
            pl.BlockSpec((9, LANES), lambda i: (0, i)),
        ),
        scratch_shapes=[padded] * 4
        + [pltpu.VMEM((TOKENS, LANES), bf16)] * 2
        + [pltpu.VMEM((TOKENS, width), f32)] * 2,
        compiler_params=params(58),
        cost_estimate=cost(12 * TOKENS * width * units, 20 << 20),
        name="ffn",
    )(*operands)


def attn_backward_kernel(
    lat_ref, po_ref, pr_ref, cot_ref, mo_ref, mr_ref, mod_ref, conv_ref, proj_ref, att_t_ref, lse_ref, wcat,
    part_ref, resid_ref, mine_ref, send_ref, sums_ref,
    low, proj_t, grads, sums,
):
    step = pl.program_id(0)
    both = wcat.shape[0] // 4
    local = both // 2
    width = wcat.shape[1]

    @pl.when(step == 0)
    def _():
        grads[...] = jnp.zeros_like(grads)
        sums[...] = jnp.zeros_like(sums)

    gate_one = mod_ref[2:3, :]
    gain = 1.0 + mod_ref[4:5, :]

    def fold(values):
        return jnp.sum(values.reshape(ROWS // 8, 8, width), 0)

    def body(j, carry):
        rows = pl.ds(pl.multiple_of(j * ROWS, ROWS), ROWS)
        attn = po_ref[rows, :].astype(f32) + pr_ref[rows, :].astype(f32)
        resid = lat_ref[rows, :].astype(f32) + gate_one * attn
        normed, scale = norm_rows(resid)
        mixed = mo_ref[rows, :].astype(f32) + mr_ref[rows, :].astype(f32)
        u = mixed * gain
        mean_u = jnp.mean(u, -1, keepdims=True)
        mean_un = jnp.mean(u * normed, -1, keepdims=True)
        grad = cot_ref[rows, :].astype(f32) + scale * (u - mean_u - normed * mean_un)
        resid_ref[rows, :] = grad
        low[rows, :] = (gate_one * grad).astype(bf16)
        sums[0] += fold(attn * grad)
        sums[1] += fold(mixed)
        sums[2] += fold(mixed * normed)
        return carry

    lax.fori_loop(0, PHASE // ROWS, body, 0)
    w_out = wcat[3 * both : 4 * both, :]
    d_att = dot_nt(low[...], w_out).astype(bf16)
    d_att_t = dot_nt(w_out, low[...]).astype(bf16)
    scale = HEAD_DIM**-0.5
    for pair in range(both // 128):
        q = proj_ref[:, pair * 128 : (pair + 1) * 128] * jnp.asarray(scale, bf16)
        k = proj_ref[:, both + pair * 128 : both + (pair + 1) * 128]
        v = proj_ref[:, 2 * both + pair * 128 : 2 * both + (pair + 1) * 128]
        d_out = d_att[:, pair * 128 : (pair + 1) * 128]
        q_t = q.T
        k_t = k.T
        for half in range(2):
            head = 2 * pair + half
            own = slice(half * HEAD_DIM, (half + 1) * HEAD_DIM)
            mask = head_mask(q.shape, half)
            scores = dot_nt(k, jnp.where(mask, q, jnp.zeros_like(q)))
            probs = jnp.exp(scores - lse_ref[head : head + 1, :])
            prob_grad = dot_nt(v, jnp.where(mask, d_out, jnp.zeros_like(d_out)))
            mean = jnp.sum(probs * prob_grad, 0, keepdims=True)
            score_grad = (probs * (prob_grad - mean)).astype(bf16)
            low_probs = probs.astype(bf16)
            d_head = d_att_t[head * HEAD_DIM : (head + 1) * HEAD_DIM, :]
            at = head * HEAD_DIM
            proj_t[at : at + HEAD_DIM, :] = (dot_nn(k_t[own, :], score_grad) * scale).astype(bf16)
            proj_t[both + at : both + at + HEAD_DIM, :] = dot_nt(q_t[own, :], score_grad).astype(bf16)
            proj_t[2 * both + at : 2 * both + at + HEAD_DIM, :] = dot_nt(d_head, low_probs).astype(bf16)
    part_ref[...] = dot_tn(proj_t[...], wcat[0 : 3 * both, :]).astype(bf16)
    grads[0 : 3 * both, :] += dot_nn(proj_t[...], conv_ref[...])
    grads[3 * both : 4 * both, :] += dot_nn(att_t_ref[...], low[...])

    @pl.when(step == pl.num_programs(0) - 1)
    def _():
        for t in range(4):
            mine_ref[t * local : (t + 1) * local, :] = grads[t * both : t * both + local, :]
            send_ref[t * local : (t + 1) * local, :] = grads[t * both + local : (t + 1) * both, :].astype(bf16)
        for t in range(3):
            sums_ref[t : t + 1, :] = jnp.sum(sums[t], 0, keepdims=True)
        sums_ref[3:8, :] = jnp.zeros((5, width), f32)


def attn_backward(lat, part_own, part_got, cot, mix_own, mix_got, mod, conv_low, proj, att_t, lse, wcat):
    both = wcat.shape[0] // 4
    width = lat.shape[1]
    block = lambda g: (g, 0)
    fixed = lambda g: (0, 0)
    token = pl.BlockSpec((PHASE, width), block)
    return pl.pallas_call(
        attn_backward_kernel,
        grid=(4,),
        out_shape=(
            jax.ShapeDtypeStruct((TOKENS, width), bf16),
            jax.ShapeDtypeStruct((TOKENS, width), f32),
            jax.ShapeDtypeStruct((2 * both, width), f32),
            jax.ShapeDtypeStruct((2 * both, width), bf16),
            jax.ShapeDtypeStruct((8, width), f32),
        ),
        in_specs=[token] * 6
        + [
            pl.BlockSpec((8, width), fixed),
            token,
            pl.BlockSpec((PHASE, 3 * both), block),
            pl.BlockSpec((None, both, PHASE), lambda g: (g, 0, 0)),
            pl.BlockSpec((None, 8, PHASE), lambda g: (g, 0, 0)),
            pl.BlockSpec((4 * both, width), fixed),
        ],
        out_specs=(
            token,
            token,
            pl.BlockSpec((2 * both, width), fixed),
            pl.BlockSpec((2 * both, width), fixed),
            pl.BlockSpec((8, width), fixed),
        ),
        scratch_shapes=[
            pltpu.VMEM((PHASE, width), bf16),
            pltpu.VMEM((3 * both, PHASE), bf16),
            pltpu.VMEM((4 * both, width), f32),
            pltpu.VMEM((3, 8, width), f32),
        ],
        compiler_params=params(58),
        cost_estimate=cost(20 * TOKENS * both * width + 20 * TOKENS * PHASE * both, 30 << 20),
        name="attn_backward",
    )(lat, part_own, part_got, cot, mix_own, mix_got, mod, conv_low, proj, att_t, lse, wcat)


def tail_kernel(
    midx_ref, lat_ref, po_ref, pr_ref, fo_ref, fr_ref, co_ref, cr_ref, cot_ref, resid_ref, mod_ref, k_ref,
    own_ref, send_ref, kg_ref, sums_ref,
    plain, shifted, grad, grad_shifted, out_low, sums,
):
    width = lat_ref.shape[1]
    zero_edges(plain, shifted, grad, grad_shifted)
    fill_shifted(lat_ref, mod_ref, plain, shifted)
    for g in range(4):

        def grad_body(row, carry):
            rows = pl.ds(pl.multiple_of(g * PHASE + row * HALF, HALF), HALF)
            values = co_ref[rows, :].astype(f32) + cr_ref[rows, :].astype(f32)
            padded = pl.ds(pl.multiple_of(HALF + row * HALF, HALF), HALF)
            grad[g, padded, :] = values
            grad_shifted[g, padded, :] = shift_columns(values, g)
            return carry

        lax.fori_loop(0, HALF, grad_body, 0)
    for first in range(0, width, LANES):
        lanes = slice(first, first + LANES)
        totals = kernel_sums(plain, shifted, grad, lanes)
        for t in range(9):
            kg_ref[t : t + 1, lanes] = jnp.sum(totals[t], 0, keepdims=True)
    for first in range(0, width, LANES):
        lanes = slice(first, first + LANES)
        flipped = spread_kernel(k_ref, lanes, True)
        for g in range(4):

            def back_body(row, carry):
                padded = pl.ds(pl.multiple_of(HALF + row * HALF, HALF), HALF)
                plain[g, padded, lanes] = conv_row(grad, grad_shifted, flipped, g, row, lanes)
                return carry

            lax.fori_loop(0, HALF, back_body, 0)
    sums[...] = jnp.zeros_like(sums)
    gate_one = mod_ref[2:3, :]
    gate_two = mod_ref[5:6, :]
    live = mod_ref[6:7, :]
    gain = 1.0 + mod_ref[1:2, :]

    def fold(values):
        return jnp.sum(values.reshape(ROWS // 8, 8, width), 0)

    for g in range(4):

        def body(j, carry):
            rows = pl.ds(pl.multiple_of(g * PHASE + j * ROWS, ROWS), ROWS)
            latent = lat_ref[rows, :].astype(f32)
            attn = po_ref[rows, :].astype(f32) + pr_ref[rows, :].astype(f32)
            ffn_out = fo_ref[rows, :].astype(f32) + fr_ref[rows, :].astype(f32)
            out = live * (latent + gate_one * attn + gate_two * ffn_out)
            out_low[0, rows, :] = out.astype(bf16)
            sums[2] += fold(ffn_out * cot_ref[rows, :].astype(f32))
            normed, scale = norm_rows(latent)
            back = plain[g, pl.ds(pl.multiple_of(HALF + j * ROWS, HALF), ROWS), :]
            u = back * gain
            mean_u = jnp.mean(u, -1, keepdims=True)
            mean_un = jnp.mean(u * normed, -1, keepdims=True)
            result = resid_ref[rows, :] + scale * (u - mean_u - normed * mean_un)
            out_low[1, rows, :] = result.astype(bf16)
            sums[0] += fold(back)
            sums[1] += fold(back * normed)
            return carry

        lax.fori_loop(0, PHASE // ROWS, body, 0)
    for t in range(3):
        sums_ref[t : t + 1, :] = jnp.sum(sums[t], 0, keepdims=True)
    sums_ref[3:8, :] = jnp.zeros((5, width), f32)
    perm = grid_permutation(True)
    for i, target in ((0, own_ref), (1, send_ref)):
        block = midx_ref[i]
        for which in range(2):
            values = jnp.concatenate(
                [
                    out_low[which, pl.ds(pl.multiple_of(g * PHASE + block * 64, 64), 64), :]
                    for g in range(4)
                ],
                0,
            )
            target[which] = dot_nn(perm, values).astype(bf16)


def tail(midx, lat, part_own, part_got, ffn_own, ffn_got, conv_own, conv_got, cot, resid, mod, kernel):
    width = lat.shape[1]
    share = jax.ShapeDtypeStruct((2, TOKENS // 4, width), bf16)
    padded = pltpu.VMEM((4, PADDED, width), f32)
    return pl.pallas_call(
        tail_kernel,
        out_shape=(
            share,
            share,
            jax.ShapeDtypeStruct((9, width), f32),
            jax.ShapeDtypeStruct((8, width), f32),
        ),
        in_specs=[SMEM] + [VMEM] * 11,
        out_specs=(VMEM,) * 4,
        scratch_shapes=[padded] * 4 + [pltpu.VMEM((2, TOKENS, width), bf16), pltpu.VMEM((3, 8, width), f32)],
        compiler_params=params(58),
        cost_estimate=cost(80 * TOKENS * width, 24 * TOKENS * width),
        name="tail",
    )(midx, lat, part_own, part_got, ffn_own, ffn_got, conv_own, conv_got, cot, resid, mod, kernel)


def ortho_kernel(inverse, left_ref, basis_ref):
    for block in range(left_ref.shape[0] // 8):
        rows = slice(8 * block, 8 * block + 8)
        factor = left_ref[rows, :] * inverse
        place = lax.broadcasted_iota(jnp.int32, (8, 1), 0)
        for k in range(8):
            products = jnp.sum(factor * factor[k : k + 1, :], -1, keepdims=True)
            scale = lax.rsqrt(products[k : k + 1, :] + ORTHO_EPS)
            column = factor[k : k + 1, :] * scale
            weight = jnp.where(place > k, products * scale, 0.0)
            factor = jnp.where(place == k, column, factor - weight * column)
        basis_ref[rows, :] = factor


def ortho(left, count):
    return pl.pallas_call(
        functools.partial(ortho_kernel, 1.0 / count),
        out_shape=jax.ShapeDtypeStruct(left.shape, f32),
        in_specs=[VMEM],
        out_specs=VMEM,
        compiler_params=params(16),
        cost_estimate=cost(left.size * 40, left.size * 8),
        name="ortho",
    )(left)


def momentum_update(weight, moment, gradient, rate):
    new_moment = MOMENTUM * moment + gradient
    return (weight - rate * new_moment, new_moment)


def per_device(
    latents, conditions, cotangent, counts, w_mod, mom_mod, conv_attn, mom_conv_attn,
    w_qkv, mom_qkv, err_qkv, start_qkv, w_out, mom_out, err_out, start_out,
    w_fc1, mom_fc1, err_fc1, start_fc1, conv_ffn, mom_conv_ffn, w_fc2, mom_fc2, err_fc2, start_fc2,
):
    slots, share, width = latents.shape
    local = w_out.shape[0]
    rank = start_out.shape[1]
    mp_count = lax.axis_size("mp")
    dp_count = lax.axis_size("dp")
    mp = lax.axis_index("mp")
    dp = lax.axis_index("dp")
    chip, core = mp // 2, mp % 2

    def swap_chip(values):
        return lax.ppermute(values, "mp", [(i, i ^ 2) for i in range(mp_count)])

    def swap_core(values):
        return lax.ppermute(values, "mp", [(i, i ^ 1) for i in range(mp_count)])

    def swap_dp(values, bit):
        return lax.ppermute(values, "dp", [(i, i ^ bit) for i in range(dp_count)])

    bits = [1 << b for b in range(dp_count.bit_length() - 1)]

    def sum_dp(values):
        for bit in bits:
            values = values + swap_dp(values, bit)
        return values

    slot = jnp.reshape(chip, (1,)).astype(jnp.int32)
    midx = jnp.stack(
        [2 * chip + core, 2 * (1 - chip) + core, 2 * chip + 1 - core, 2 * (1 - chip) + 1 - core]
    ).astype(jnp.int32)

    own_l, own_c, snd_l, snd_c = enter(slot, latents, cotangent)
    got_l = swap_chip(snd_l)
    sib_own_l = swap_core(own_l)
    sib_got_l = swap_core(got_l)
    lat_pieces = (own_l, got_l, sib_own_l, sib_got_l)

    silu_own = jax.nn.silu(conditions.astype(f32)).astype(bf16)
    silu_all = lax.all_to_all(silu_own, "dp", split_axis=1, concat_axis=0, tiled=True)
    silu_all = silu_all.reshape(dp_count, slots, -1)
    silu_slot = lax.dynamic_index_in_dim(silu_all, chip, 1, keepdims=False)
    partial = jnp.dot(silu_slot, w_mod.astype(bf16), preferred_element_type=f32)
    gathered = lax.all_to_all(partial, "dp", split_axis=0, concat_axis=0, tiled=True)
    modulation = jnp.sum(gathered, 0).reshape(6, width)
    live = (counts[0] > chip).astype(f32)
    mod = jnp.concatenate([modulation, jnp.full((2, width), live, f32)], 0)

    def fetch(shard):
        rows = shard.shape[0] // 2
        place = dp % 2
        half = lax.dynamic_slice_in_dim(shard, place * rows, rows, 0)
        near = swap_chip(half)
        far = swap_dp(near, 1)
        return jnp.where(place == 0, jnp.concatenate([near, far], 0), jnp.concatenate([far, near], 0))

    attn_a = pack_attn(w_qkv, w_out)
    attn_b = fetch(attn_a)
    fc1_a, fc2_a = w_fc1.astype(bf16), w_fc2.astype(bf16)
    got_c = swap_chip(snd_c)
    sib_own_c = swap_core(own_c)
    sib_got_c = swap_core(got_c)
    cot_pieces = (own_c, got_c, sib_own_c, sib_got_c)
    both_b = fetch(jnp.concatenate([fc1_a, fc2_a], 0))
    fc1_b, fc2_b = both_b[: fc1_a.shape[0]], both_b[fc1_a.shape[0] :]
    conv_ffn_b = swap_chip(conv_ffn)

    lat, conv_low = first_conv(midx, lat_pieces, mod, conv_attn)
    wcat, proj, att_t, lse, part = attn_forward(conv_low, attn_a, attn_b)
    part_got = swap_core(part)
    mixed, mixed_t, fgl, cot = second_norm(midx, lat, part, part_got, cot_pieces, mod)
    ffn_a, mix_a, grad_fc1, grad_fc2, kgrad_a = ffn(mixed, mixed_t, fgl, fc1_a, fc2_a, conv_ffn, None, f32)
    ffn_part, mix_part, snd_fc1, snd_fc2, kgrad_b = ffn(
        mixed, mixed_t, fgl, fc1_b, fc2_b, conv_ffn_b, (ffn_a, mix_a), bf16
    )
    mix_got = swap_core(mix_part)
    ffn_got = swap_core(ffn_part)
    got_fc2 = swap_chip(snd_fc2)
    got_fc1 = swap_chip(snd_fc1)
    kgrad_got = swap_chip(kgrad_b)
    conv_part, resid_grad, grad_attn, snd_attn, sums_two = attn_backward(
        lat, part, part_got, cot, mix_part, mix_got, mod, conv_low, proj, att_t, lse, wcat
    )
    got_attn = swap_chip(snd_attn)
    conv_got = swap_core(conv_part)
    own_out, snd_out, kgrad_attn, sums_one = tail(
        midx, lat, part, part_got, ffn_part, ffn_got, conv_part, conv_got, cot, resid_grad, mod, conv_attn
    )
    got_out = swap_chip(snd_out)
    outs = jnp.where(chip == 0, jnp.stack([own_out, got_out], 1), jnp.stack([got_out, own_out], 1))

    mod_total = jnp.concatenate([sums_one[0:2], sums_two[0:3], sums_one[2:3]], 0).reshape(1, -1)
    for bit in bits:
        mod_total = jnp.concatenate([mod_total, swap_dp(mod_total, bit)], 0)
    other_total = swap_chip(mod_total)
    count = jnp.arange(dp_count)
    pick = ((dp ^ count)[:, None] == count[None, :]).astype(bf16)
    silu_order = jnp.dot(pick, silu_all.reshape(dp_count, -1)).reshape(silu_all.shape)
    totals = jnp.where(
        chip == 0, jnp.concatenate([mod_total, other_total], 0), jnp.concatenate([other_total, mod_total], 0)
    )
    mod_mean = (
        jnp.dot(
            jnp.concatenate([silu_order[:, s] for s in range(slots)], 0).astype(f32).T,
            totals,
            precision=HIGHEST,
            preferred_element_type=f32,
        )
        / dp_count
    )
    w_mod_new, mom_mod_new = momentum_update(w_mod, mom_mod, mod_mean, LEARN_RATE)

    merged_attn = grad_attn + got_attn.astype(f32)
    merged_qkv = merged_attn[: 3 * local].reshape(3, local, width).transpose(0, 2, 1) + err_qkv[0]
    merged_out = merged_attn[3 * local :] + err_out[0]
    merged_fc1 = grad_fc1 + got_fc1.astype(f32) + err_fc1[0]
    merged_fc2 = grad_fc2 + got_fc2.astype(f32) + err_fc2[0]
    left_qkv = jnp.einsum("tdo,tor->rd", merged_qkv, start_qkv, precision=HIGHEST)
    left_out = jnp.einsum("cd,dr->rc", merged_out, start_out, precision=HIGHEST)
    left_fc1 = jnp.einsum("df,fr->rd", merged_fc1, start_fc1, precision=HIGHEST)
    left_fc2 = jnp.einsum("fd,dr->rf", merged_fc2, start_fc2, precision=HIGHEST)
    left = jnp.concatenate(
        [left_qkv, left_fc1, left_fc2, jnp.pad(left_out, ((0, 0), (0, width - local)))], 0
    )
    left = sum_dp(left)
    basis = ortho(left, dp_count)
    basis_qkv, basis_fc1, basis_fc2 = basis[:rank], basis[rank : 2 * rank], basis[2 * rank : 3 * rank]
    basis_out = basis[3 * rank :, :local]
    right_qkv = jnp.einsum("tdo,rd->tro", merged_qkv, basis_qkv, precision=HIGHEST)
    right_out = jnp.einsum("cd,rc->rd", merged_out, basis_out, precision=HIGHEST)
    right_fc1 = jnp.einsum("df,rd->rf", merged_fc1, basis_fc1, precision=HIGHEST)
    right_fc2 = jnp.einsum("fd,rf->rd", merged_fc2, basis_fc2, precision=HIGHEST)
    kgrad_chip = kgrad_attn + swap_chip(kgrad_attn)
    rights = jnp.concatenate(
        [
            right_out,
            right_fc1,
            right_fc2,
            jnp.pad(right_qkv.transpose(1, 0, 2).reshape(rank, -1), ((0, 0), (0, width - 3 * local))),
            kgrad_chip,
            kgrad_a + kgrad_got,
        ],
        0,
    )
    rights = sum_dp(rights) / dp_count
    right_out, right_fc1, right_fc2 = rights[:rank], rights[rank : 2 * rank], rights[2 * rank : 3 * rank]
    right_qkv = rights[3 * rank : 4 * rank, : 3 * local].reshape(rank, 3, local)
    conv_attn_new, mom_conv_attn_new = momentum_update(
        conv_attn, mom_conv_attn, rights[4 * rank : 4 * rank + 9], LEARN_RATE
    )
    conv_ffn_new, mom_conv_ffn_new = momentum_update(
        conv_ffn, mom_conv_ffn, rights[4 * rank + 9 : 4 * rank + 18], FAST_RATE
    )
    approx_qkv = jnp.einsum("rd,rto->tdo", basis_qkv, right_qkv, precision=HIGHEST)
    approx_out = jnp.einsum("rc,rd->cd", basis_out, right_out, precision=HIGHEST)
    approx_fc1 = jnp.einsum("rd,rf->df", basis_fc1, right_fc1, precision=HIGHEST)
    approx_fc2 = jnp.einsum("rf,rd->fd", basis_fc2, right_fc2, precision=HIGHEST)
    w_qkv_new, mom_qkv_new = momentum_update(w_qkv, mom_qkv, approx_qkv, LEARN_RATE)
    w_out_new, mom_out_new = momentum_update(w_out, mom_out, approx_out, FAST_RATE)
    w_fc1_new, mom_fc1_new = momentum_update(w_fc1, mom_fc1, approx_fc1, LEARN_RATE)
    w_fc2_new, mom_fc2_new = momentum_update(w_fc2, mom_fc2, approx_fc2, LEARN_RATE)
    return (
        outs[0], outs[1], w_mod_new, mom_mod_new, conv_attn_new, mom_conv_attn_new,
        w_qkv_new, mom_qkv_new, (merged_qkv - approx_qkv)[None],
        w_out_new, mom_out_new, (merged_out - approx_out)[None],
        w_fc1_new, mom_fc1_new, (merged_fc1 - approx_fc1)[None],
        conv_ffn_new, mom_conv_ffn_new,
        w_fc2_new, mom_fc2_new, (merged_fc2 - approx_fc2)[None],
    )


def solution(mesh):
    token = P("dp", "mp", None)
    rows = P("mp", None)
    columns = P(None, "mp")
    placed = (
        token, P("dp", None), token, P("dp"), P("dp", None), P("dp", None), P(), P(),
        P(None, None, "mp"), P(None, None, "mp"), P("dp", None, None, "mp"), P(None, "mp", None),
        rows, rows, P("dp", "mp", None), P(),
        columns, columns, P("dp", None, "mp"), rows,
        columns, columns,
        rows, rows, P("dp", "mp", None), P(),
    )
    results = (
        token, token, P("dp", None), P("dp", None), P(), P(),
        P(None, None, "mp"), P(None, None, "mp"), P("dp", None, None, "mp"),
        rows, rows, P("dp", "mp", None),
        columns, columns, P("dp", None, "mp"),
        columns, columns,
        rows, rows, P("dp", "mp", None),
    )
    return jax.shard_map(per_device, mesh=mesh, in_specs=placed, out_specs=results, check_vma=False)
```

time: 1200 us -> 392 us (0.33)
  other arithmetic: 388 us -> 19.4 us
  waiting for transfers between devices: 417 us -> 98.3 us
  Pallas kernels: 0 us -> 154 us
  local copies, waits for them, and re-layouts: 145 us -> 28.9 us
  matrix products: 144 us -> 45.1 us
  blocking collectives: 48.7 us -> 0 us
  between operations: 40.1 us -> 2.29 us
  starting transfers between devices: 1.45 us -> 38.9 us
    reduce_sum x82 -> x1, other arithmetic: 182 us -> 0.11 us  [per_device(): modulation = jnp.sum(gathered, 0).reshape(6, width)]
    psum x4 -> x0, waiting for transfers between devices: 176 us -> none  [the longest x1 62.9 us: per_device(): lax.psum(attn_part.astype(jnp.bfloat16), 'mp').astype(jnp.float32)]
    pallas_call x0 -> x10, Pallas kernels: none -> 154 us  [the longest x2 57.9 us: ffn(): pl.pallas_call(functools.partial(ffn_kernel, first), grid=(units // LANES...]
    all_gather x3 -> x0, waiting for transfers between devices: 130 us -> none  [the longest x1 102 us: per_device(): lax.all_gather(w_mod.astype(jnp.bfloat16), 'dp', axis=0, tiled=True)]
    reduce_scatter x3 -> x0, waiting for transfers between devices: 110 us -> none  [the longest x1 110 us: per_device(): lax.psum_scatter(mod_full_grad.astype(jnp.bfloat16), 'dp', scatter_dimens...]
    mul x11 -> x0, other arithmetic: 94.4 us -> none  [the longest x7 70.3 us: orthonormal(): current * lax.rsqrt(jnp.sum(current * current, -1, keepdims=True) + ORTHO...]
    dot_general x48 -> x15, matrix products: 139 us -> 45.1 us  [the longest x1 9.5 us: per_device(): jnp.einsum('rf,rd->fd', basis_fc2, right_fc2, precision=HIGHEST)]
    ppermute x0 -> x31, waiting for transfers between devices: none -> 84.8 us  [the longest x12 63.9 us: swap_chip(): return lax.ppermute(values, 'mp', [(i, i ^ 2) for i in range(mp_count)])]
  transfers between devices with their start and end apart: 10 -> 33, of which waited for: 7 -> 16; matrix products, arithmetic and copies ran while one was open for 43% -> 18% of each run, Pallas kernels for 0% -> 24%
where the time goes in v1:
time: 392 us; the launch traced here: 387 us
  Pallas kernels  154 us (39%)
  waiting for transfers between devices  98.3 us (25%)
  matrix products  45.1 us (12%)
  starting transfers between devices  38.9 us (10%)
  local copies, waits for them, and re-layouts  28.9 us (7%)
  other arithmetic  19.4 us (5%)
    ppermute x12, waiting for transfers between devices, swap_chip(): return lax.ppermute(values, 'mp', [(i, i ^ 2) for i in range(mp_count)])  63.9 us
    pallas_call x2, Pallas kernels, ffn(): pl.pallas_call(functools.partial(ffn_kernel, first), grid=(units // LANES...  57.9 us
    pallas_call x1, Pallas kernels, attn_backward(): pl.pallas_call(attn_backward_kernel, grid=(4,), out_shape=(jax.ShapeDtype...  32.1 us
    pallas_call x1, Pallas kernels, tail(): pl.pallas_call(tail_kernel, out_shape=(share, share, jax.ShapeDtypeStruct...  30.2 us
    ppermute x11, waiting for transfers between devices, swap_dp(): return lax.ppermute(values, 'dp', [(i, i ^ bit) for i in range(dp_count)])  19.7 us
    ppermute x12, starting transfers between devices, swap_chip(): return lax.ppermute(values, 'mp', [(i, i ^ 2) for i in range(mp_count)])  16.8 us
    unnamed x122, local copies, waits for them, and re-layouts  16.6 us
    pallas_call x1, Pallas kernels, attn_forward(): pl.pallas_call(attn_forward_kernel, grid=(4,), out_shape=(jax.ShapeDtypeS...  13.5 us
  transfers between devices with their start and end apart: 33, of which 16 were waited for; matrix products, arithmetic and copies ran while one was open for 18% of the time, Pallas kernels for 24%

profile of v1, /device:TPU:0, one launch (start us, length us, event | category | flops | bytes accessed | tf_op | source)
XLA Modules:
  0.0 387.1 jit_solution(18331784670945133827)
XLA Ops:
  0.7 2.0 copy.68.qkv_ref
  5.2 2.9 collective-permute-start.3
  8.1 1.9 convert_element_type.37.w1_ref
  11.9 2.3 fusion.2
  16.3 2.0 collective-permute-start
  18.3 4.2 %collective-permute-done.3 = bf16[384,768]{1,0:T(8,128)(2,1)} collective-permute-done((bf16[384,768]{1,0:T(8,128)(2,1)}, bf16[384,768]{1,0:T(8,128)(2,1)}, u32[]{:S(2)}, u32[]{:S(2)}) %collective-permute-start.3) | collective-permute-done | bytes 589856 | tf_op jit(solution)/shard_map/ppermute | solution.py:751
  22.6 2.1 collective-permute-start.4
  25.4 4.9 %all-to-all-start = ((bf16[2,8,96]{2,0,1:T(2,128)(2,1)}), bf16[2,8,96]{2,0,1:T(2,128)(2,1)S(1)}, u32[]{:S(2)}, u32[]{:S(2)}) async-start(bf16[2,8,96]{2,0,1:T(2,128)(2,1)} %copy.65), calls=%async_computation | async-start | bytes 8192 | tf_op jit(solution)/shard_map/all_to_all | solution.py:778
  30.3 6.4 %all-to-all-done = bf16[2,8,96]{2,0,1:T(2,128)(2,1)S(1)} async-done(((bf16[2,8,96]{2,0,1:T(2,128)(2,1)}), bf16[2,8,96]{2,0,1:T(2,128)(2,1)S(1)}, u32[]{:S(2)}, u32[]{:S(2)}) %all-to-all-start) | async-done | bytes 3104 | tf_op jit(solution)/shard_map/all_to_all | solution.py:778
  36.7 18.7 %collective-permute-done.p1 = bf16[256,768]{1,0:T(8,128)(2,1)S(1)} collective-permute-done((bf16[256,768]{1,0:T(8,128)(2,1)S(1)}, bf16[256,768]{1,0:T(8,128)(2,1)S(1)}, u32[]{:S(2)}, u32[]{:S(2)}) %collective-permute-start) | collective-permute-done | bytes 393248 | tf_op jit(solution)/shard_map/ppermute | solution.py:751
  55.3 1.7 convolution_bitcast_fusion
  57.9 6.3 %all-to-all-start.1 = ((f32[8,1,4608]{2,1,0:T(1,128)}), f32[8,1,4608]{2,1,0:T(1,128)S(1)}, u32[]{:S(2)}, u32[]{:S(2)}) async-start(f32[8,1,4608]{2,1,0:T(1,128)} %copy.67), calls=%async_computation.1 | async-start | bytes 294912 | tf_op jit(solution)/shard_map/all_to_all | solution.py:782
  64.9 7.1 %all-to-all-done.1 = f32[8,1,4608]{2,1,0:T(1,128)S(1)} async-done(((f32[8,1,4608]{2,1,0:T(1,128)}), f32[8,1,4608]{2,1,0:T(1,128)S(1)}, u32[]{:S(2)}, u32[]{:S(2)}) %all-to-all-start.1) | async-done | bytes 147488 | tf_op jit(solution)/shard_map/all_to_all | solution.py:782
  72.2 10.4 %first_conv.1 = (bf16[1024,768]{1,0:T(8,128)(2,1)S(1)}, bf16[1024,768]{1,0:T(8,128)(2,1)S(1)}) custom-call(s32[4]{0:T(128)S(1)} %pad_add_fusion.midx_ref, bf16[256,768]{1,0:T(8,128)(2,1)S(1)} %get-tuple-element.54.p0, bf16[256,768]{1,0:T(8,128)(2,1)S(1)} %collective-permute-done.p1, bf16[256,768]{1,0:T(8,128)(2,1)S(1)} %collective-permute-done.1.p2, ...), custom_call_target="tpu_custom_call" | custom-call | flops 23592960 | bytes 4718592 | tf_op jit(solution)/shard_map/first_conv/pallas_call | solution.py:236
  84.0 1.9 maximum_select_fusion.2.wb_ref
  85.9 13.5 %attn_forward.1 = (bf16[1536,768]{1,0:T(8,128)(2,1)}, bf16[1024,1152]{1,0:T(8,128)(2,1)}, bf16[4,384,256]{2,1,0:T(8,128)(2,1)S(1)}, f32[4,8,256]{2,1,0:T(8,128)S(1)}, bf16[1024,768]{1,0:T(8,128)(2,1)S(1)}) custom-call(bf16[1024,768]{1,0:T(8,128)(2,1)} %copy-done.18, bf16[768,768]{1,0:T(8,128)(2,1)S(1)} %copy-done.6, ...), custom_call_target="tpu_custom_call" | custom-call | flops 3221225472 | bytes 16777216 | tf_op jit(solution)/shard_map/attn_forward/pallas_call | solution.py:288
  101.7 9.9 %collective-permute-done.6.c1 = bf16[256,768]{1,0:T(8,128)(2,1)S(1)} collective-permute-done((bf16[256,768]{1,0:T(8,128)(2,1)S(1)}, bf16[256,768]{1,0:T(8,128)(2,1)S(1)}, u32[]{:S(2)}, u32[]{:S(2)}) %collective-permute-start.6) | collective-permute-done | bytes 393248 | tf_op jit(solution)/shard_map/ppermute | solution.py:751
  111.6 2.0 maximum_select_fusion
  115.2 8.1 %second_norm.1 = (bf16[1024,768]{1,0:T(8,128)(2,1)S(1)}, bf16[768,1024]{1,0:T(8,128)(2,1)S(1)}, bf16[1024,768]{1,0:T(8,128)(2,1)S(1)}, bf16[1024,768]{1,0:T(8,128)(2,1)S(1)}) custom-call(s32[4]{0:T(128)S(1)} %pad_add_fusion.midx_ref, bf16[1024,768]{1,0:T(8,128)(2,1)S(1)} %get-tuple-element.56.lat_ref, bf16[1024,768]{1,0:T(8,128)(2,1)S(1)} %get-tuple-element.58.po_ref, ...), custom_call_target="tpu_custom_call" | custom-call | flops 15728640 | bytes 12582912 | tf_op jit(solution)/shard_map/second_norm/pallas_call | solution.py:342
  128.0 28.6 %ffn.2 = (f32[1024,768]{1,0:T(8,128)}, f32[1024,768]{1,0:T(8,128)}, f32[768,768]{1,0:T(8,128)}, f32[768,768]{1,0:T(8,128)}, f32[9,768]{1,0:T(8,128)}) custom-call(bf16[1024,768]{1,0:T(8,128)(2,1)} %copy-done.19, bf16[768,1024]{1,0:T(8,128)(2,1)} %copy-done.20, bf16[1024,768]{1,0:T(8,128)(2,1)} %copy-done.21, bf16[768,768]{1,0:T(8,128)(2,1)} %copy-done.37, ...), custom_call_target="tpu_custom_call" | custom-call | flops 7247757312 | bytes 20971520 | tf_op jit(solution)/shard_map/ffn/pallas_call | solution.py:451
  157.2 29.3 %ffn.3 = (bf16[1024,768]{1,0:T(8,128)(2,1)}, bf16[1024,768]{1,0:T(8,128)(2,1)}, bf16[768,768]{1,0:T(8,128)(2,1)}, bf16[768,768]{1,0:T(8,128)(2,1)}, f32[9,768]{1,0:T(8,128)}) custom-call(bf16[1024,768]{1,0:T(8,128)(2,1)} %copy-done.19, bf16[768,1024]{1,0:T(8,128)(2,1)} %copy-done.20, bf16[1024,768]{1,0:T(8,128)(2,1)} %copy-done.21, ...), custom_call_target="tpu_custom_call" | custom-call | flops 7247757312 | bytes 20971520 | tf_op jit(solution)/shard_map/ffn/pallas_call | solution.py:451
  191.5 32.1 %attn_backward.1 = (bf16[1024,768]{1,0:T(8,128)(2,1)}, f32[1024,768]{1,0:T(8,128)}, f32[768,768]{1,0:T(8,128)}, bf16[768,768]{1,0:T(8,128)(2,1)}, f32[8,768]{1,0:T(8,128)}) custom-call(bf16[1024,768]{1,0:T(8,128)(2,1)} %copy-done.2, bf16[1024,768]{1,0:T(8,128)(2,1)} %copy-done.3, bf16[1024,768]{1,0:T(8,128)(2,1)} %copy-done.4, bf16[1024,768]{1,0:T(8,128)(2,1)} %copy-done.9, ...), custom_call_target="tpu_custom_call" | custom-call | flops 8053063680 | bytes 31457280 | tf_op jit(solution)/shard_map/attn_backward/pallas_call | solution.py:563
  226.2 2.7 bitcast_add_fusion.1
  228.9 2.0 convolution_bitcast_fusion.3
  230.9 10.6 %collective-permute-done.22 = bf16[768,768]{1,0:T(8,128)(2,1)} collective-permute-done((bf16[768,768]{1,0:T(8,128)(2,1)}, bf16[768,768]{1,0:T(8,128)(2,1)}, u32[]{:S(2)}, u32[]{:S(2)}) %collective-permute-start.22) | collective-permute-done | bytes 1179680 | tf_op jit(solution)/shard_map/ppermute | solution.py:751
  241.5 1.8 bitcast_add_fusion
  243.3 2.0 convolution_bitcast_fusion.2
  245.3 20.4 %collective-permute-done.20 = bf16[768,768]{1,0:T(8,128)(2,1)S(1)} collective-permute-done((bf16[768,768]{1,0:T(8,128)(2,1)}, bf16[768,768]{1,0:T(8,128)(2,1)S(1)}, u32[]{:S(2)}, u32[]{:S(2)}) %collective-permute-start.20) | collective-permute-done | bytes 1179680 | tf_op jit(solution)/shard_map/ppermute | solution.py:751
  266.3 2.6 copy-done.30
  272.3 3.1 collective-permute-done.23
  278.0 2.2 collective-permute-done.24
  281.0 5.8 %collective-permute-done.25 = f32[32,768]{1,0:T(8,128)S(1)} collective-permute-done((f32[32,768]{1,0:T(8,128)S(1)}, f32[32,768]{1,0:T(8,128)S(1)}, u32[]{:S(2)}, u32[]{:S(2)}) %collective-permute-start.25) | collective-permute-done | bytes 98336 | tf_op jit(solution)/shard_map/ppermute | solution.py:757
  287.7 3.5 fusion.20
  291.2 30.2 %tail.1 = (bf16[2,256,768]{2,1,0:T(8,128)(2,1)}, bf16[2,256,768]{2,1,0:T(8,128)(2,1)}, f32[9,768]{1,0:T(8,128)}, f32[8,768]{1,0:T(8,128)}) custom-call(s32[4]{0:T(128)} %copy-done.17, bf16[1024,768]{1,0:T(8,128)(2,1)} %copy-done.2, bf16[1024,768]{1,0:T(8,128)(2,1)} %copy-done.3, bf16[1024,768]{1,0:T(8,128)(2,1)} %copy-done.4, ...), custom_call_target="tpu_custom_call" | custom-call | flops 62914560 | bytes 18874368 | tf_op jit(solution)/shard_map/tail/pallas_call | solution.py:688
  327.4 1.8 fusion.18
  332.9 2.1 fusion.22
  335.2 1.8 concatenate.63
  337.8 1.6 collective-permute-start.19
  339.4 3.0 collective-permute-done.28
  346.3 2.3 concatenate.60
  348.7 1.8 collective-permute-done.29
  352.2 5.1 %multiply_subtract_fusion.3 = (f32[96,4608]{1,0:T(8,128)}, f32[96,4608]{1,0:T(8,128)}) fusion(f32[96,4608]{1,0:T(8,128)} %param.30, f32[16,4608]{1,0:T(8,128)} %concatenate.60, f32[16,4608]{1,0:T(8,128)S(1)} %concatenate.61, pred[]{:T(512)S(6)} %eq.25, bf16[8,96]{1,0:T(8,128)(2,1)S(1)} %get-tuple-element.111, bf16[8,96]{1,0:T(8,128)(2,1)S(1)} %get-tuple-element.110, ...), kind=kOutput, calls=%fused_computation.20 | convolution fusion | flops 87226368 | bytes 7670785 | tf_op jit(solution)/shard_map/dot_general | solution.py:841
  357.3 2.0 collective-permute-done.30
  359.4 3.5 fusion.8
  362.8 3.2 multiply_subtract_fusion.4
  366.9 7.5 %multiply_subtract_fusion.2 = (f32[3,768,192]{1,2,0:T(8,128)}, f32[3,768,192]{1,2,0:T(8,128)}, f32[1,3,768,192]{2,3,1,0:T(8,128)}) fusion(f32[3,768,192]{1,2,0:T(8,128)} %param.34, f32[3,768,192]{1,2,0:T(8,128)} %param.35, f32[3,768,192]{1,2,0:T(8,128)} %bitcast.92, f32[1,3,768,192]{2,3,1,0:T(8,128)} %param.36, f32[32,768]{1,0:T(8,128)S(1)} %ortho.1, ...), kind=kOutput, calls=%fused_computation.19 | convolution fusion | flops 45121536 | bytes 12443648 | tf_op jit(solution)/shard_map/rd,rto->tdo/dot_general | solution.py:892
  374.4 9.5 %multiply_subtract_fusion = (f32[768,768]{1,0:T(8,128)}, f32[768,768]{1,0:T(8,128)}, f32[1,768,768]{2,1,0:T(8,128)}, f32[1,768,768]{2,1,0:T(8,128)}, f32[768,768]{1,0:T(8,128)}, /*index=5*/f32[768,768]{1,0:T(8,128)}) fusion(f32[768,768]{1,0:T(8,128)S(1)} %copy-done.34, f32[768,768]{1,0:T(8,128)S(1)} %copy-done.38, f32[768,768]{1,0:T(8,128)S(1)} %copy-done.28, ...), kind=kOutput, calls=%fused_computation.9 | convolution fusion | flops 62521344 | bytes 30720000 | tf_op jit(solution)/shard_map/rf,rd->fd/dot_general | solution.py:895
  383.9 1.7 maximum_select_fusion.1
  (216 shorter events, 52.3 us)
Async XLA Ops:
  0.7 228.2 %copy-start = (f32[768,8]{0,1:T(8,128)S(1)}, f32[768,8]{0,1:T(8,128)}, u32[]{:S(2)}) copy-start(f32[768,8]{0,1:T(8,128)} %param.45) | copy-start | bytes 73732
  5.2 17.4 %collective-permute-start.3 = (bf16[384,768]{1,0:T(8,128)(2,1)}, bf16[384,768]{1,0:T(8,128)(2,1)}, u32[]{:S(2)}, u32[]{:S(2)}) collective-permute-start(bf16[384,768]{1,0:T(8,128)(2,1)} %constant_dynamic-slice_fusion), channel_id=1, source_target_pairs={{0,2},{1,3},{2,0},{3,1},{4,6},{5,7},{6,4},{7,5},{8,10},{9,11},{10,... | collective-permute-start | bytes 1769480 | tf_op jit(solution)/shard_map/ppermute | solution.py:751
  14.2 69.5 %collective-permute-start.9 = (bf16[768,768]{1,0:T(8,128)(2,1)}, bf16[768,768]{1,0:T(8,128)(2,1)}, u32[]{:S(2)}, u32[]{:S(2)}) collective-permute-start(bf16[768,768]{1,0:T(8,128)(2,1)} %fusion.2), channel_id=1, source_target_pairs={{0,2},{1,3},{2,0},{3,1},{4,6},{5,7},{6,4},{7,5},{8,10},{9,11},{10,... | collective-permute-start | bytes 3538952 | tf_op jit(solution)/shard_map/ppermute | solution.py:751
  16.3 55.9 %copy-start.12 = (f32[9,768]{1,0:T(8,128)S(1)}, f32[9,768]{1,0:T(8,128)}, u32[]{:S(2)}) copy-start(f32[9,768]{1,0:T(8,128)} %k_ref.5) | copy-start | bytes 82948
  16.3 39.0 %collective-permute-start = (bf16[256,768]{1,0:T(8,128)(2,1)S(1)}, bf16[256,768]{1,0:T(8,128)(2,1)S(1)}, u32[]{:S(2)}, u32[]{:S(2)}) collective-permute-start(bf16[256,768]{1,0:T(8,128)(2,1)S(1)} %get-tuple-element.55), channel_id=1, source_target_pairs={{0,2},{1,3},{2,0},{3,1},{4,6},{5,7},{6,4},{7,5},{8,10},{9,11},{10,... | collective-permute-start | bytes 1179656 | tf_op jit(solution)/shard_map/ppermute | solution.py:751
  22.6 61.4 %collective-permute-start.4 = (bf16[384,768]{1,0:T(8,128)(2,1)}, bf16[384,768]{1,0:T(8,128)(2,1)S(1)}, u32[]{:S(2)}, u32[]{:S(2)}) collective-permute-start(bf16[384,768]{1,0:T(8,128)(2,1)} %collective-permute-done.3), channel_id=1, source_target_pairs={{0,4},{4,0},{8,12},{12,8},{16,20},{20,16},{24,28},{28,24},{1,5},{5... | collective-permute-start | bytes 1769480 | tf_op jit(solution)/shard_map/ppermute | solution.py:757
  25.4 11.3 %all-to-all-start = ((bf16[2,8,96]{2,0,1:T(2,128)(2,1)}), bf16[2,8,96]{2,0,1:T(2,128)(2,1)S(1)}, u32[]{:S(2)}, u32[]{:S(2)}) async-start(bf16[2,8,96]{2,0,1:T(2,128)(2,1)} %copy.65), calls=%async_computation | async-start | bytes 8192 | tf_op jit(solution)/shard_map/all_to_all | solution.py:778
  30.3 41.9 %collective-permute-start.1 = (bf16[256,768]{1,0:T(8,128)(2,1)S(1)}, bf16[256,768]{1,0:T(8,128)(2,1)S(1)}, u32[]{:S(2)}, u32[]{:S(2)}) collective-permute-start(bf16[256,768]{1,0:T(8,128)(2,1)S(1)} %get-tuple-element.54.p0), channel_id=1, source_target_pairs={{0,1},{1,0},{2,3},{3,2},{4,5},{5,4},{6,7},{7,6},{8,9},{9,8},{10,11... | collective-permute-start | bytes 1179656 | tf_op jit(solution)/shard_map/ppermute | solution.py:754
  55.3 16.8 %collective-permute-start.2 = (bf16[256,768]{1,0:T(8,128)(2,1)S(1)}, bf16[256,768]{1,0:T(8,128)(2,1)S(1)}, u32[]{:S(2)}, u32[]{:S(2)}) collective-permute-start(bf16[256,768]{1,0:T(8,128)(2,1)S(1)} %collective-permute-done.p1), channel_id=1, source_target_pairs={{0,1},{1,0},{2,3},{3,2},{4,5},{5,4},{6,7},{7,6},{8,9},{9,8},{10,11... | collective-permute-start | bytes 1179656 | tf_op jit(solution)/shard_map/ppermute | solution.py:754
  57.9 14.1 %all-to-all-start.1 = ((f32[8,1,4608]{2,1,0:T(1,128)}), f32[8,1,4608]{2,1,0:T(1,128)S(1)}, u32[]{:S(2)}, u32[]{:S(2)}) async-start(f32[8,1,4608]{2,1,0:T(1,128)} %copy.67), calls=%async_computation.1 | async-start | bytes 294912 | tf_op jit(solution)/shard_map/all_to_all | solution.py:782
  64.9 50.2 %copy-start.17 = (s32[4]{0:T(128)}, s32[4]{0:T(128)S(1)}, u32[]{:S(2)}) copy-start(s32[4]{0:T(128)S(1)} %pad_add_fusion.midx_ref) | copy-start | bytes 52
  72.1 43.0 %copy-start.14 = (f32[8,768]{1,0:T(8,128)}, f32[8,768]{1,0:T(8,128)S(1)}, u32[]{:S(2)}) copy-start(f32[8,768]{1,0:T(8,128)S(1)} %concatenate.49.mod_ref) | copy-start | bytes 73732
  83.7 31.4 %copy-start.2 = (bf16[1024,768]{1,0:T(8,128)(2,1)}, bf16[1024,768]{1,0:T(8,128)(2,1)S(1)}, u32[]{:S(2)}) copy-start(bf16[1024,768]{1,0:T(8,128)(2,1)S(1)} %get-tuple-element.56.lat_ref) | copy-start | bytes 4718596
  83.7 27.8 %collective-permute-start.10 = (bf16[768,768]{1,0:T(8,128)(2,1)}, bf16[768,768]{1,0:T(8,128)(2,1)S(1)}, u32[]{:S(2)}, u32[]{:S(2)}) collective-permute-start(bf16[768,768]{1,0:T(8,128)(2,1)} %collective-permute-done.9), channel_id=1, source_target_pairs={{0,4},{4,0},{8,12},{12,8},{16,20},{20,16},{24,28},{28,24},{1,5},{5... | collective-permute-start | bytes 3538952 | tf_op jit(solution)/shard_map/ppermute | solution.py:757
  85.9 15.2 %copy-start.48 = (f32[9,768]{1,0:T(8,128)S(1)}, f32[9,768]{1,0:T(8,128)}, u32[]{:S(2)}) copy-start(f32[9,768]{1,0:T(8,128)} %k_ref.4) | copy-start | bytes 82948
  85.9 15.7 %copy-start.16 = (bf16[256,768]{1,0:T(8,128)(2,1)S(1)}, bf16[256,768]{1,0:T(8,128)(2,1)}, u32[]{:S(2)}) copy-start(bf16[256,768]{1,0:T(8,128)(2,1)} %copy-done.15) | copy-start | bytes 1179652
  99.5 14.1 %copy-start.24 = (bf16[4,384,256]{2,1,0:T(8,128)(2,1)}, bf16[4,384,256]{2,1,0:T(8,128)(2,1)S(1)}, u32[]{:S(2)}) copy-start(bf16[4,384,256]{2,1,0:T(8,128)(2,1)S(1)} %get-tuple-element.70.att_t_ref) | copy-start | bytes 2359300
  99.5 14.1 %copy-start.25 = (f32[4,8,256]{2,1,0:T(8,128)}, f32[4,8,256]{2,1,0:T(8,128)S(1)}, u32[]{:S(2)}) copy-start(f32[4,8,256]{2,1,0:T(8,128)S(1)} %get-tuple-element.71.lse_ref) | copy-start | bytes 98308
  99.5 15.7 %copy-start.3 = (bf16[1024,768]{1,0:T(8,128)(2,1)}, bf16[1024,768]{1,0:T(8,128)(2,1)S(1)}, u32[]{:S(2)}) copy-start(bf16[1024,768]{1,0:T(8,128)(2,1)S(1)} %get-tuple-element.58.po_ref) | copy-start | bytes 4718596
  99.5 15.6 %collective-permute-start.5 = (bf16[1024,768]{1,0:T(8,128)(2,1)S(1)}, bf16[1024,768]{1,0:T(8,128)(2,1)S(1)}, u32[]{:S(2)}, u32[]{:S(2)}) collective-permute-start(bf16[1024,768]{1,0:T(8,128)(2,1)S(1)} %get-tuple-element.58.po_ref), channel_id=1, source_target_pairs={{0,1},{1,0},{2,3},{3,2},{4,5},{5,4},{6,7},{7,6},{8,9},{9,8},{10,11... | collective-permute-start | bytes 4718600 | tf_op jit(solution)/shard_map/ppermute | solution.py:754
  99.6 12.0 %collective-permute-start.6 = (bf16[256,768]{1,0:T(8,128)(2,1)S(1)}, bf16[256,768]{1,0:T(8,128)(2,1)S(1)}, u32[]{:S(2)}, u32[]{:S(2)}) collective-permute-start(bf16[256,768]{1,0:T(8,128)(2,1)S(1)} %copy-done.23), channel_id=1, source_target_pairs={{0,2},{1,3},{2,0},{3,1},{4,6},{5,7},{6,4},{7,5},{8,10},{9,11},{10,... | collective-permute-start | bytes 1179656 | tf_op jit(solution)/shard_map/ppermute | solution.py:751
  101.1 55.4 %collective-permute-start.11 = (f32[9,768]{1,0:T(8,128)S(1)}, f32[9,768]{1,0:T(8,128)S(1)}, u32[]{:S(2)}, u32[]{:S(2)}) collective-permute-start(f32[9,768]{1,0:T(8,128)S(1)} %copy-done.48), channel_id=1, source_target_pairs={{0,2},{1,3},{2,0},{3,1},{4,6},{5,7},{6,4},{7,5},{8,10},{9,11},{10,... | collective-permute-start | bytes 82952 | tf_op jit(solution)/shard_map/ppermute | solution.py:751
  101.7 13.5 %collective-permute-start.7 = (bf16[256,768]{1,0:T(8,128)(2,1)S(1)}, bf16[256,768]{1,0:T(8,128)(2,1)S(1)}, u32[]{:S(2)}, u32[]{:S(2)}) collective-permute-start(bf16[256,768]{1,0:T(8,128)(2,1)S(1)} %copy-done.16), channel_id=1, source_target_pairs={{0,1},{1,0},{2,3},{3,2},{4,5},{5,4},{6,7},{7,6},{8,9},{9,8},{10,11... | collective-permute-start | bytes 1179656 | tf_op jit(solution)/shard_map/ppermute | solution.py:754
  111.5 3.6 collective-permute-start.8
  186.5 3.8 collective-permute-start.13
  187.1 38.1 %collective-permute-start.21 = (bf16[768,768]{1,0:T(8,128)(2,1)}, bf16[768,768]{1,0:T(8,128)(2,1)S(1)}, u32[]{:S(2)}, u32[]{:S(2)}) collective-permute-start(bf16[768,768]{1,0:T(8,128)(2,1)} %get-tuple-element.82), channel_id=1, source_target_pairs={{0,2},{1,3},{2,0},{3,1},{4,6},{5,7},{6,4},{7,5},{8,10},{9,11},{10,... | collective-permute-start | bytes 3538952 | tf_op jit(solution)/shard_map/ppermute | solution.py:751
  188.6 52.9 %collective-permute-start.22 = (bf16[768,768]{1,0:T(8,128)(2,1)}, bf16[768,768]{1,0:T(8,128)(2,1)}, u32[]{:S(2)}, u32[]{:S(2)}) collective-permute-start(bf16[768,768]{1,0:T(8,128)(2,1)} %get-tuple-element.84), channel_id=1, source_target_pairs={{0,2},{1,3},{2,0},{3,1},{4,6},{5,7},{6,4},{7,5},{8,10},{9,11},{10,... | collective-permute-start | bytes 3538952 | tf_op jit(solution)/shard_map/ppermute | solution.py:751
  189.1 102.1 %collective-permute-start.12 = (bf16[1024,768]{1,0:T(8,128)(2,1)}, bf16[1024,768]{1,0:T(8,128)(2,1)}, u32[]{:S(2)}, u32[]{:S(2)}) collective-permute-start(bf16[1024,768]{1,0:T(8,128)(2,1)} %get-tuple-element.66.fo_ref), channel_id=1, source_target_pairs={{0,1},{1,0},{2,3},{3,2},{4,5},{5,4},{6,7},{7,6},{8,9},{9,8},{10,11... | collective-permute-start | bytes 4718600 | tf_op jit(solution)/shard_map/ppermute | solution.py:754
  191.5 34.7 %copy-start.39 = (f32[1,768,768]{2,1,0:T(8,128)S(1)}, f32[1,768,768]{2,1,0:T(8,128)}, u32[]{:S(2)}) copy-start(f32[1,768,768]{2,1,0:T(8,128)} %param.44) | copy-start | bytes 7077892
  223.6 42.2 %collective-permute-start.20 = (bf16[768,768]{1,0:T(8,128)(2,1)}, bf16[768,768]{1,0:T(8,128)(2,1)S(1)}, u32[]{:S(2)}, u32[]{:S(2)}) collective-permute-start(bf16[768,768]{1,0:T(8,128)(2,1)} %get-tuple-element.80), channel_id=1, source_target_pairs={{0,2},{1,3},{2,0},{3,1},{4,6},{5,7},{6,4},{7,5},{8,10},{9,11},{10,... | collective-permute-start | bytes 3538952 | tf_op jit(solution)/shard_map/ppermute | solution.py:751
  226.2 15.3 %copy-start.41 = (f32[768,768]{1,0:T(8,128)S(1)}, f32[768,768]{1,0:T(8,128)}, u32[]{:S(2)}) copy-start(f32[768,768]{1,0:T(8,128)} %get-tuple-element.83) | copy-start | bytes 7077892
  243.3 22.9 %copy-start.26 = (f32[768,768]{1,0:T(8,128)}, f32[768,768]{1,0:T(8,128)S(1)}, u32[]{:S(2)}) copy-start(f32[768,768]{1,0:T(8,128)S(1)} %bitcast_add_fusion) | copy-start | bytes 7077892
  243.3 22.5 %copy-start.42 = (f32[768,768]{1,0:T(8,128)S(1)}, f32[768,768]{1,0:T(8,128)}, u32[]{:S(2)}) copy-start(f32[768,768]{1,0:T(8,128)} %get-tuple-element.79) | copy-start | bytes 7077892
  245.3 45.9 %collective-permute-start.14 = (bf16[1024,768]{1,0:T(8,128)(2,1)}, bf16[1024,768]{1,0:T(8,128)(2,1)}, u32[]{:S(2)}, u32[]{:S(2)}) collective-permute-start(bf16[1024,768]{1,0:T(8,128)(2,1)} %get-tuple-element.73.co_ref), channel_id=1, source_target_pairs={{0,1},{1,0},{2,3},{3,2},{4,5},{5,4},{6,7},{7,6},{8,9},{9,8},{10,11... | collective-permute-start | bytes 4718600 | tf_op jit(solution)/shard_map/ppermute | solution.py:754
  270.8 4.7 %collective-permute-start.23 = (f32[32,768]{1,0:T(8,128)S(1)}, f32[32,768]{1,0:T(8,128)S(1)}, u32[]{:S(2)}, u32[]{:S(2)}) collective-permute-start(f32[32,768]{1,0:T(8,128)S(1)} %select_maximum_fusion), channel_id=1, source_target_pairs={{0,4},{4,0},{8,12},{12,8},{16,20},{20,16},{24,28},{28,24},{1,5},{5... | collective-permute-start | bytes 294920 | tf_op jit(solution)/shard_map/ppermute | solution.py:757
  275.5 4.7 %collective-permute-start.24 = (f32[32,768]{1,0:T(8,128)S(1)}, f32[32,768]{1,0:T(8,128)S(1)}, u32[]{:S(2)}, u32[]{:S(2)}) collective-permute-start(f32[32,768]{1,0:T(8,128)S(1)} %fusion.36), channel_id=1, source_target_pairs={{0,8},{4,12},{8,0},{12,4},{16,24},{20,28},{24,16},{28,20},{1,9},{5... | collective-permute-start | bytes 294920 | tf_op jit(solution)/shard_map/ppermute | solution.py:757
  276.5 4.5 %collective-permute-start.27 = (f32[9,768]{1,0:T(8,128)S(1)}, f32[9,768]{1,0:T(8,128)S(1)}, u32[]{:S(2)}, u32[]{:S(2)}) collective-permute-start(f32[9,768]{1,0:T(8,128)S(1)} %copy-done.58), channel_id=1, source_target_pairs={{0,2},{1,3},{2,0},{3,1},{4,6},{5,7},{6,4},{7,5},{8,10},{9,11},{10,... | collective-permute-start | bytes 82952 | tf_op jit(solution)/shard_map/ppermute | solution.py:751
  280.2 6.6 %collective-permute-start.25 = (f32[32,768]{1,0:T(8,128)S(1)}, f32[32,768]{1,0:T(8,128)S(1)}, u32[]{:S(2)}, u32[]{:S(2)}) collective-permute-start(f32[32,768]{1,0:T(8,128)S(1)} %add.126), channel_id=1, source_target_pairs={{0,16},{4,20},{8,24},{12,28},{16,0},{20,4},{24,8},{28,12},{1,17},{... | collective-permute-start | bytes 294920 | tf_op jit(solution)/shard_map/ppermute | solution.py:757
  291.2 32.8 %copy-start.27 = (f32[768,768]{1,0:T(8,128)S(1)}, f32[768,768]{1,0:T(8,128)}, u32[]{:S(2)}) copy-start(f32[768,768]{1,0:T(8,128)} %copy-done.26) | copy-start | bytes 7077892
  323.0 3.8 collective-permute-start.16
  326.8 4.0 %collective-permute-start.17 = (f32[2,4608]{1,0:T(2,128)S(1)}, f32[2,4608]{1,0:T(2,128)S(1)}, u32[]{:S(2)}, u32[]{:S(2)}) collective-permute-start(f32[2,4608]{1,0:T(2,128)S(1)} %pad_maximum_fusion.2), channel_id=1, source_target_pairs={{0,8},{4,12},{8,0},{12,4},{16,24},{20,28},{24,16},{28,20},{1,9},{5... | collective-permute-start | bytes 110600 | tf_op jit(solution)/shard_map/ppermute | solution.py:757
  329.3 5.9 %collective-permute-start.26 = (f32[9,768]{1,0:T(8,128)S(1)}, f32[9,768]{1,0:T(8,128)S(1)}, u32[]{:S(2)}, u32[]{:S(2)}) collective-permute-start(f32[9,768]{1,0:T(8,128)S(1)} %copy-done.47), channel_id=1, source_target_pairs={{0,2},{1,3},{2,0},{3,1},{4,6},{5,7},{6,4},{7,5},{8,10},{9,11},{10,... | collective-permute-start | bytes 82952 | tf_op jit(solution)/shard_map/ppermute | solution.py:751
  331.6 6.2 %collective-permute-start.18 = (f32[4,4608]{1,0:T(4,128)}, f32[4,4608]{1,0:T(4,128)S(1)}, u32[]{:S(2)}, u32[]{:S(2)}) collective-permute-start(f32[4,4608]{1,0:T(4,128)} %pad_maximum_fusion.1), channel_id=1, source_target_pairs={{0,16},{4,20},{8,24},{12,28},{16,0},{20,4},{24,8},{28,12},{1,17},{... | collective-permute-start | bytes 221192 | tf_op jit(solution)/shard_map/ppermute | solution.py:757
  337.0 5.5 %collective-permute-start.28 = (f32[50,768]{1,0:T(8,128)S(1)}, f32[50,768]{1,0:T(8,128)S(1)}, u32[]{:S(2)}, u32[]{:S(2)}) collective-permute-start(f32[50,768]{1,0:T(8,128)S(1)} %concatenate.63), channel_id=1, source_target_pairs={{0,4},{4,0},{8,12},{12,8},{16,20},{20,16},{24,28},{28,24},{1,5},{5... | collective-permute-start | bytes 460808 | tf_op jit(solution)/shard_map/ppermute | solution.py:757
  337.8 7.5 %collective-permute-start.19 = (f32[8,4608]{1,0:T(8,128)S(1)}, f32[8,4608]{1,0:T(8,128)}, u32[]{:S(2)}, u32[]{:S(2)}) collective-permute-start(f32[8,4608]{1,0:T(8,128)S(1)} %pad_maximum_fusion), channel_id=1, source_target_pairs={{0,2},{1,3},{2,0},{3,1},{4,6},{5,7},{6,4},{7,5},{8,10},{9,11},{10,... | collective-permute-start | bytes 442376 | tf_op jit(solution)/shard_map/ppermute | solution.py:751
  343.1 7.3 %collective-permute-start.29 = (f32[50,768]{1,0:T(8,128)}, f32[50,768]{1,0:T(8,128)}, u32[]{:S(2)}, u32[]{:S(2)}) collective-permute-start(f32[50,768]{1,0:T(8,128)} %add.130), channel_id=1, source_target_pairs={{0,8},{4,12},{8,0},{12,4},{16,24},{20,28},{24,16},{28,20},{1,9},{5... | collective-permute-start | bytes 460808 | tf_op jit(solution)/shard_map/ppermute | solution.py:757
  343.8 40.2 %collective-permute-start.15 = (bf16[2,256,768]{2,1,0:T(8,128)(2,1)}, bf16[2,256,768]{2,1,0:T(8,128)(2,1)}, u32[]{:S(2)}, u32[]{:S(2)}) collective-permute-start(bf16[2,256,768]{2,1,0:T(8,128)(2,1)} %get-tuple-element.76), channel_id=1, source_target_pairs={{0,2},{1,3},{2,0},{3,1},{4,6},{5,7},{6,4},{7,5},{8,10},{9,11},{10,... | collective-permute-start | bytes 2359304 | tf_op jit(solution)/shard_map/ppermute | solution.py:751
  351.5 7.9 %collective-permute-start.30 = (f32[50,768]{1,0:T(8,128)S(1)}, f32[50,768]{1,0:T(8,128)S(1)}, u32[]{:S(2)}, u32[]{:S(2)}) collective-permute-start(f32[50,768]{1,0:T(8,128)S(1)} %add.131), channel_id=1, source_target_pairs={{0,16},{4,20},{8,24},{12,28},{16,0},{20,4},{24,8},{28,12},{1,17},{... | collective-permute-start | bytes 460808 | tf_op jit(solution)/shard_map/ppermute | solution.py:757
  (45 other events, 207.7 us)
